TPU v7x, 32 devices: a whole 2x2x4 slice. The times are simulated.
32 devices in a mesh: gx: 4 (over x, core), ev: 8 (over z, y).
Axes of the slice: x: 2, y: 2, z: 4, core: 2. Of those that a mesh axis runs over, the one named last changes fastest.
Arguments:
- partial_kernels: bfloat16 [8, 2048, 2, 8, 2048], P('ev', 'gx'), may hold values from -8 to 8
- illumination: float32 [2048, 8, 2048], P('gx', None, 'ev'), may hold values from 0.3 to 3
- classes_x: int32 [8, 2048], P(None, 'ev'), may hold values from 0 to 2
- classes_y: int32 [2048, 8], P('gx'), may hold values from 0 to 2
- widths_x: float32 [3], replicated, may hold values from 0.5 to 1
- widths_y: float32 [3], replicated, may hold values from 0.5 to 1
Outputs:
- conditioned: bfloat16 [2048, 2, 8, 2048], P('gx', None, None, 'ev')
All inputs are finite; a program needn't handle non-finite values.
Results may differ from a plain program's by a relative error of at most 0.0035.
Values may be sent and summed in bfloat16 or wider, within the bound.
No kernel may reach another device: no remote copies, remote signals or barrier semaphores. Data moves between devices by JAX's collectives and lax.ppermute only.
A program may use at most 192 MiB of HBM per device.

v0:
```python
import jax
import jax.numpy as jnp
from jax import lax
from jax.sharding import PartitionSpec as P

BAND = 128


blend_weight = 0.25
soft_bound = 2.0


def with_halo(shard, sides, width):
    for axis, dim in sides:
        size, length = (lax.axis_size(axis), shard.shape[dim])
        up = [(i, (i + 1) % size) for i in range(size - 1)]
        down = [(j, i) for i, j in up]
        last = lax.slice_in_dim(shard, length - width, length, axis=dim)
        initial = lax.slice_in_dim(shard, 0, width, axis=dim)
        before = lax.ppermute(last, axis, up)
        after = lax.ppermute(initial, axis, down)
        shard = jnp.concatenate([before, shard, after], axis=dim)
    return shard


def smoother_window(length, fraction, first_row, rows, cols):
    row_pos = first_row + jnp.arange(rows, dtype=jnp.float32)
    col_pos = first_row - BAND + jnp.arange(cols, dtype=jnp.float32)
    offset = row_pos[:, None] - col_pos[None, :]
    inside = (jnp.abs(offset) <= BAND) & (col_pos[None, :] >= 0.0) & (col_pos[None, :] < length)
    distance = offset / (fraction * BAND)
    gaussian = jnp.where(inside, jnp.exp(-0.5 * distance * distance), jnp.float32(0.0))
    gaussian = gaussian / jnp.sum(gaussian, axis=1, keepdims=True)
    diagonal = jnp.where(offset == 0.0, jnp.float32(blend_weight), jnp.float32(0.0))
    return (gaussian + diagonal).astype(jnp.bfloat16)


def smooth_columns(columns, labels, matrices):
    summed = jnp.zeros((matrices[0].shape[0], columns.shape[1]), jnp.float32)
    for level in range(len(matrices)):
        product = jnp.dot(matrices[level], columns, preferred_element_type=jnp.float32)
        summed = summed + jnp.where(labels[None, :] == level, product, jnp.float32(0.0))
    return summed


def smooth_rows(row_block, labels, matrices):
    summed = jnp.zeros((row_block.shape[0], matrices[0].shape[0]), jnp.float32)
    for level in range(len(matrices)):
        product = lax.dot_general(
            row_block, matrices[level], (((1,), (1,)), ((), ())), preferred_element_type=jnp.float32
        )
        summed = summed + jnp.where(labels[:, None] == level, product, jnp.float32(0.0))
    return summed


def per_device(partial_kernels, illumination, classes_x, classes_y, widths_x, widths_y):
    own_part = partial_kernels[0]
    slab_x, kernels, planes, full_y = own_part.shape
    groups = lax.axis_size("ev")
    owners = lax.axis_size("gx")
    slab_y = full_y // groups
    full_x = slab_x * owners
    count_levels = widths_x.shape[0]
    summed = lax.psum_scatter(
        own_part.astype(jnp.float32).astype(jnp.bfloat16), "ev", scatter_dimension=3, tiled=True
    ).astype(jnp.float32)
    scaled = (summed / illumination[:, None, :, :]).astype(jnp.bfloat16)
    widened_x = with_halo(scaled, (("gx", 0),), BAND)
    first_x = (lax.axis_index("gx") * slab_x).astype(jnp.float32)
    windows_x = [
        smoother_window(full_x, widths_x[level], first_x, slab_x, slab_x + 2 * BAND)
        for level in range(count_levels)
    ]
    labels_x = jnp.broadcast_to(classes_x[None, :, :], (kernels, planes, slab_y)).reshape(-1)
    smoothed_x = smooth_columns(widened_x.reshape(slab_x + 2 * BAND, -1), labels_x, windows_x)
    bounded = (
        (soft_bound * jnp.tanh(smoothed_x / soft_bound))
        .astype(jnp.bfloat16)
        .reshape(slab_x, kernels, planes, slab_y)
    )
    widened_y = with_halo(bounded, (("ev", 3),), BAND)
    first_y = (lax.axis_index("ev") * slab_y).astype(jnp.float32)
    windows_y = [
        smoother_window(full_y, widths_y[level], first_y, slab_y, slab_y + 2 * BAND)
        for level in range(count_levels)
    ]
    labels_y = jnp.broadcast_to(classes_y[:, None, :], (slab_x, kernels, planes)).reshape(-1)
    smoothed_y = smooth_rows(widened_y.reshape(-1, slab_y + 2 * BAND), labels_y, windows_y)
    conditioned = smoothed_y.astype(jnp.bfloat16).reshape(slab_x, kernels, planes, slab_y)
    return conditioned


def solution(mesh):
    return jax.shard_map(
        per_device,
        mesh=mesh,
        in_specs=(
            P("ev", "gx", None, None, None),
            P("gx", None, "ev"),
            P(None, "ev"),
            P("gx", None),
            P(),
            P(),
        ),
        out_specs=P("gx", None, None, "ev"),
        check_vma=False,
    )
```

profile of v0, /device:TPU:1, one launch (start us, length us, event | category | flops | bytes accessed | tf_op | source)
XLA Modules:
  0.0 728.6 jit_solution(7571238795193833949)
XLA Ops:
  6.5 0.0 reduce-scatter.2.cloned.1.call-start
  6.5 0.0 copy-start.4
  6.5 0.7 reduce-scatter.2.cloned.1.call-update
  7.3 0.0 copy-done.4
  7.3 0.6 fusion.107
  9.6 0.0 copy-done.3
  9.7 546.8 %reduce-scatter.2.cloned.1.call-done = bf16[512,2,8,256]{3,2,1,0:T(8,128)(2,1)} async-done(((bf16[512,2,8,2048]{3,2,1,0:T(8,128)(2,1)}), bf16[512,2,8,256]{3,2,1,0:T(8,128)(2,1)}) %reduce-scatter.2.cloned.1.call-update) | async-done | bytes 4194320 | tf_op jit(solution)/shard_map/reduce_scatter | solution.py:64
  556.5 5.1 divide_convert_fusion
  561.6 0.1 fusion.106
  561.8 3.5 collective-permute-start
  565.3 1.9 collective-permute-start.1
  567.2 1.9 fusion.48
  569.2 7.8 %collective-permute-done = bf16[128,2,8,256]{3,2,1,0:T(8,128)(2,1)S(1)} collective-permute-done((bf16[128,2,8,256]{3,2,1,0:T(8,128)(2,1)S(1)}, bf16[128,2,8,256]{3,2,1,0:T(8,128)(2,1)S(1)}, u32[]{:S(2)}, u32[]{:S(2)}) %collective-permute-start) | collective-permute-done | bytes 1048608 | tf_op jit(solution)/shard_map/ppermute | solution.py:20
  577.0 4.4 collective-permute-done.1
  581.4 7.3 pad_maximum_fusion.1
  588.6 4.2 copy.16
  592.9 6.9 fusion.18
  599.8 6.9 fusion.16
  606.7 9.7 %multiply_convert_fusion = bf16[512,4096]{1,0:T(8,128)(2,1)S(1)} fusion(f32[512,4096]{1,0:T(8,128)} %fusion.16, f32[512,4096]{1,0:T(8,128)} %fusion.18, bf16[768,4096]{1,0:T(8,128)(2,1)S(1)} %bitcast.25, pred[4096]{0:T(1024)(128)(4,1)S(1)} %eq.112, pred[4096]{0:T(1024)(128)(4,1)S(1)} %eq.109, pred[4096]{0:T(1024)(128)(4,1)S(1)} %eq.105, ...), kind=kOutput, calls=%fused_computation.7 | convolution fusion | flops 3243507712 | bytes 27283972 | tf_op jit(solution)/shard_map/dot_general | solution.py:41
  616.4 0.0 copy-start
  616.4 1.4 copy.17
  617.9 0.6 copy-done
  618.4 0.0 copy-start.5
  618.4 0.0 copy-start.2
  618.4 2.1 fusion.105
  620.5 4.4 collective-permute-start.2
  625.0 1.3 collective-permute-start.3
  626.2 0.0 copy-done.5
  626.3 0.7 fusion.108
  628.8 0.0 copy-done.2
  628.8 0.2 copy.14
  629.0 0.2 broadcast_in_dim.145
  629.2 0.5 eq.116
  629.7 0.2 copy.13
  629.9 0.2 broadcast_in_dim.131
  630.1 0.5 eq.102
  630.6 0.2 copy.15
  630.8 0.2 broadcast_in_dim.147
  631.0 0.5 eq.119
  631.5 0.7 fusion.72
  632.2 7.6 %concatenate.15 = bf16[8192,256]{1,0:T(8,128)(2,1)} reshape(bf16[512,4096]{1,0:T(8,128)(2,1)} %copy-done) | data formatting | bytes 8388608 | tf_op jit(solution)/shard_map/concatenate | solution.py:22
  639.9 63.3 %collective-permute-done.2 = bf16[512,2,8,128]{3,2,1,0:T(8,128)(2,1)} collective-permute-done((bf16[512,2,8,128]{3,2,1,0:T(8,128)(2,1)}, bf16[512,2,8,128]{3,2,1,0:T(8,128)(2,1)}, u32[]{:S(2)}, u32[]{:S(2)}) %collective-permute-start.2) | collective-permute-done | bytes 2097184 | tf_op jit(solution)/shard_map/ppermute | solution.py:20
  703.2 0.0 collective-permute-done.3
  703.2 0.0 copy-start.1
  703.2 5.6 convolution_select_fusion.1
  708.8 0.0 copy-done.1
  708.8 5.0 fusion.2
  713.8 7.9 %fusion.1 = bf16[8192,256]{1,0:T(8,128)(2,1)} fusion(f32[8192,256]{1,0:T(8,128)S(1)} %fusion.2, pred[8192]{0:T(1024)(128)(4,1)S(1)} %eq.119, f32[256]{0:T(256)S(1)} %get-tuple-element.8, f32[512]{0:T(512)S(1)} %iota_add_fusion.1, f32[256]{0:T(256)S(1)} %iota_add_fusion.3, f32[]{:T(128)} %bitcast.8, pred[512]{0:T(512)(128)(4,1)S(1)} %get-tuple-element.27, ...), kind=kOutput, calls=%fused_computation.2 | convolution fusion | flops 2180775936 | bytes 20984836 | tf_op jit(solution)/shard_map/dot_general | solution.py:49
  (15 shorter events, 0.1 us)
Async XLA Ops:
  6.5 550.0 %reduce-scatter.2.cloned.1.call-start = ((), (), s32[]{:S(2)}) async-start(), calls=%async_computation.1 | async-start | bytes 37748736 | tf_op jit(solution)/shard_map/reduce_scatter | solution.py:64
  6.5 0.7 copy-start.4
  6.5 3.1 copy-start.3
  561.8 15.2 %collective-permute-start = (bf16[128,2,8,256]{3,2,1,0:T(8,128)(2,1)S(1)}, bf16[128,2,8,256]{3,2,1,0:T(8,128)(2,1)S(1)}, u32[]{:S(2)}, u32[]{:S(2)}) collective-permute-start(bf16[128,2,8,256]{3,2,1,0:T(8,128)(2,1)S(1)} %get-tuple-element.13), channel_id=1, source_target_pairs={{0,8},{8,16},{16,24},{1,9},{9,17},{17,25},{2,10},{10,18},{18,26},{... | collective-permute-start | bytes 3145736 | tf_op jit(solution)/shard_map/ppermute | solution.py:20
  565.3 16.1 %collective-permute-start.1 = (bf16[128,2,8,256]{3,2,1,0:T(8,128)(2,1)S(1)}, bf16[128,2,8,256]{3,2,1,0:T(8,128)(2,1)S(1)}, u32[]{:S(2)}, u32[]{:S(2)}) collective-permute-start(bf16[128,2,8,256]{3,2,1,0:T(8,128)(2,1)S(1)} %get-tuple-element.14), channel_id=1, source_target_pairs={{8,0},{16,8},{24,16},{9,1},{17,9},{25,17},{10,2},{18,10},{26,18},{... | collective-permute-start | bytes 3145736 | tf_op jit(solution)/shard_map/ppermute | solution.py:21
  616.4 2.0 copy-start
  618.4 7.8 %copy-start.5 = (f32[3]{0:T(128)S(1)}, f32[3]{0:T(128)}, u32[]{:S(2)}) copy-start(f32[3]{0:T(128)} %param.11) | copy-start | bytes 40
  618.4 10.4 %copy-start.2 = (s32[512,8]{0,1:T(8,128)S(1)}, s32[512,8]{0,1:T(8,128)}, u32[]{:S(2)}) copy-start(s32[512,8]{0,1:T(8,128)} %param.9) | copy-start | bytes 49156
  620.5 82.7 %collective-permute-start.2 = (bf16[512,2,8,128]{3,2,1,0:T(8,128)(2,1)}, bf16[512,2,8,128]{3,2,1,0:T(8,128)(2,1)}, u32[]{:S(2)}, u32[]{:S(2)}) collective-permute-start(bf16[512,2,8,128]{3,2,1,0:T(8,128)(2,1)} %get-tuple-element.11), channel_id=1, source_target_pairs={{0,1},{1,2},{2,3},{3,4},{4,5},{5,6},{6,7},{8,9},{9,10},{10,11},{11... | collective-permute-start | bytes 6291464 | tf_op jit(solution)/shard_map/ppermute | solution.py:20
  625.0 78.2 %collective-permute-start.3 = (bf16[512,2,8,128]{3,2,1,0:T(8,128)(2,1)S(1)}, bf16[512,2,8,128]{3,2,1,0:T(8,128)(2,1)}, u32[]{:S(2)}, u32[]{:S(2)}) collective-permute-start(bf16[512,2,8,128]{3,2,1,0:T(8,128)(2,1)S(1)} %get-tuple-element.12), channel_id=1, source_target_pairs={{1,0},{2,1},{3,2},{4,3},{5,4},{6,5},{7,6},{9,8},{10,9},{11,10},{12... | collective-permute-start | bytes 6291464 | tf_op jit(solution)/shard_map/ppermute | solution.py:21
  703.2 5.6 copy-start.1
Sparse Core Ops, SparseCore 0:
  11.1 545.3 reduce-scatter.1
where the time goes:
time: 729 us
  waiting for transfers between devices  623 us (85%)
  matrix products  42.1 us (6%)
  local copies, waits for them, and re-layouts  20 us (3%)
  between operations  17.3 us (2%)
  other arithmetic  15.1 us (2%)
  starting transfers between devices  11.1 us (2%)
    reduce_scatter x1, waiting for transfers between devices, per_device(): lax.psum_scatter(own_part.astype(jnp.float32).astype(jnp.bfloat16), 'ev',...  547 us
    ppermute x2, waiting for transfers between devices, with_halo(): before = lax.ppermute(last, axis, up)  71.2 us
    dot_general x3, matrix products, smooth_columns(): jnp.dot(matrices[level], columns, preferred_element_type=jnp.float32)  23.5 us
    dot_general x3, matrix products, smooth_rows(): lax.dot_general(row_block, matrices[level], (((1,), (1,)), ((), ())), pre...  18.5 us
  transfers between devices with their start and end apart: 5, of which 4 were waited for; matrix products, arithmetic and copies ran while one was open for 2% of the time, Pallas kernels for 0%

commit v1 on v0

v1 whole, which is shorter than its diff:
```python
import functools

import jax
import jax.numpy as jnp
from jax import lax
from jax.experimental import pallas as pl
from jax.experimental.pallas import tpu as pltpu
from jax.sharding import PartitionSpec as P

BAND = 128
PAIR = 2

blend_weight = 0.25
soft_bound = 2.0


def plan_chunks(kernels, half):
    lead = half // 2
    chunks = [("zy", 0, 0, lead), ("yz", 0, lead, half - lead)]
    for k in range(1, kernels):
        chunks.append(("yz", k, 0, lead))
        chunks += [("yz", k, j, 1) for j in range(lead, half)]
    return chunks


VMEM = 60 * 1024 * 1024


def params():
    return pltpu.CompilerParams(vmem_limit_bytes=VMEM)


def cost(flops, nbytes, trans=0):
    return pl.CostEstimate(flops=int(flops), bytes_accessed=int(nbytes), transcendentals=int(trans))


def split_planes(own_part, perm, kernel_id, chunks, shards, rows, after=()):
    _, slab_x, _, planes, full_y = own_part.shape
    half = planes // PAIR
    wide = full_y // shards
    span = perm.shape[0]
    sub = span // planes
    outs, specs, plan = [], [], []
    for order, _, first, slots in chunks:
        parts = ((0, half),) if order == "zy" else ((0,), (half,))
        for offsets in parts:
            count = slots * len(offsets)
            outs.append(jax.ShapeDtypeStruct((shards, count, slab_x, wide), jnp.bfloat16))
            specs.append(pl.BlockSpec((1, count, rows, wide), lambda s, i: (s, 0, i, 0)))
            plan.append([offset + first + j for offset in offsets for j in range(slots)])

    def body(part_ref, perm_ref, *refs):
        out_refs = refs[len(after) :]
        for b in range(rows // sub):
            block = part_ref[0, b * sub : (b + 1) * sub, 0].astype(jnp.float32)
            block = block.reshape(span, wide).astype(jnp.bfloat16)
            moved = jnp.dot(perm_ref[...], block, preferred_element_type=jnp.float32)
            moved = moved.astype(jnp.bfloat16).reshape(planes, sub, wide)
            for out_ref, slots_of in zip(out_refs, plan):
                for n, q in enumerate(slots_of):
                    out_ref[0, n, b * sub : (b + 1) * sub, :] = moved[q]

    return pl.pallas_call(
        body,
        grid=(shards, slab_x // rows),
        in_specs=[
            pl.BlockSpec((1, rows, 1, planes, wide), lambda s, i: (0, i, kernel_id, 0, s)),
            pl.BlockSpec(perm.shape, lambda s, i: (0, 0)),
        ]
        + [pl.BlockSpec(memory_space=pl.ANY)] * len(after),
        out_specs=specs,
        out_shape=outs,
        compiler_params=params(),
        cost_estimate=cost(0, 0),
        name="split_planes",
    )(own_part, perm, *after)


def hold(array, after):
    def body(*refs):
        del refs

    anywhere = pl.BlockSpec(memory_space=pl.ANY)
    return pl.pallas_call(
        body,
        in_specs=[anywhere] * (1 + len(after)),
        out_specs=anywhere,
        out_shape=jax.ShapeDtypeStruct(array.shape, array.dtype),
        input_output_aliases={0: 0},
        compiler_params=params(),
        cost_estimate=cost(0, 0),
        name="hold",
    )(array, *after)


def add_parts(a, b, after=()):
    shards, slots, slab_x, wide = a.shape

    def body(a_ref, b_ref, *refs):
        out_ref = refs[-1]
        out_ref[...] = (a_ref[...].astype(jnp.float32) + b_ref[...].astype(jnp.float32)).astype(jnp.bfloat16)

    spec = pl.BlockSpec((1, 1, slab_x, wide), lambda s, m: (s, m, 0, 0))
    return pl.pallas_call(
        body,
        grid=(shards, slots),
        in_specs=[spec, spec] + [pl.BlockSpec(memory_space=pl.ANY)] * len(after),
        out_specs=spec,
        out_shape=jax.ShapeDtypeStruct(a.shape, jnp.bfloat16),
        compiler_params=params(),
        cost_estimate=cost(a.size, 6 * a.size),
        name="add_parts",
    )(a, b, *after)


def scale(terms, lit, lit_pair, place, first, after=()):
    slots, slab_x, wide = terms[0].shape
    narrow = wide // PAIR
    count = len(terms)

    def body(place_ref, *refs):
        term_refs, (lit_ref, pair_ref) = refs[:count], refs[count : count + 2]
        out_ref, top_ref, bottom_ref = refs[-3:]
        left = place_ref[0] == 0
        for h in range(PAIR):
            total = term_refs[0][0, :, h * narrow : (h + 1) * narrow].astype(jnp.float32)
            for ref in term_refs[1:]:
                total = total + ref[0, :, h * narrow : (h + 1) * narrow].astype(jnp.float32)
            mine, theirs = lit_ref[0], pair_ref[0].astype(jnp.float32)
            by = jnp.where(left, mine, theirs) if h == 0 else jnp.where(left, theirs, mine)
            out_ref[0, :, h * narrow : (h + 1) * narrow] = (total / by).astype(jnp.bfloat16)
        top_ref[0] = out_ref[0, :BAND]
        bottom_ref[0] = out_ref[0, slab_x - BAND :]

    full = pl.BlockSpec((1, slab_x, wide), lambda m, place_ref: (m, 0, 0))
    edge = pl.BlockSpec((1, BAND, wide), lambda m, place_ref: (m, 0, 0))
    lit_spec = pl.BlockSpec((1, slab_x, narrow), lambda m, place_ref: (first + m, 0, 0))
    size = slots * slab_x * wide
    return pl.pallas_call(
        body,
        grid_spec=pltpu.PrefetchScalarGridSpec(
            num_scalar_prefetch=1,
            grid=(slots,),
            in_specs=[full] * count + [lit_spec, lit_spec] + [pl.BlockSpec(memory_space=pl.ANY)] * len(after),
            out_specs=[full, edge, edge],
        ),
        out_shape=[
            jax.ShapeDtypeStruct((slots, slab_x, wide), jnp.bfloat16),
            jax.ShapeDtypeStruct((slots, BAND, wide), jnp.bfloat16),
            jax.ShapeDtypeStruct((slots, BAND, wide), jnp.bfloat16),
        ],
        compiler_params=params(),
        cost_estimate=cost(size * 4, size * (2 * count + 6)),
        name="scale",
    )(place, *terms, lit, lit_pair, *after)


def band_tiles(length, widths, first, tiles, rows):
    shape = (widths.shape[0], tiles, rows, rows + 2 * BAND)
    base = first + rows * lax.broadcasted_iota(jnp.int32, shape, 1)
    row_pos = base + lax.broadcasted_iota(jnp.int32, shape, 2)
    col_pos = base - BAND + lax.broadcasted_iota(jnp.int32, shape, 3)
    offset = (row_pos - col_pos).astype(jnp.float32)
    inside = (jnp.abs(offset) <= BAND) & (col_pos >= 0) & (col_pos < length)
    distance = offset / (widths[:, None, None, None] * BAND)
    gaussian = jnp.where(inside, jnp.exp(-0.5 * distance * distance), jnp.float32(0.0))
    gaussian = gaussian / jnp.sum(gaussian, axis=3, keepdims=True)
    diagonal = jnp.where(offset == 0.0, jnp.float32(blend_weight), jnp.float32(0.0))
    return (gaussian + diagonal).astype(jnp.bfloat16)


def smooth_x(scaled, before, after, tiles_x, labels, first):
    slots, slab_x, wide = scaled.shape
    classes, tiles, rows, window = tiles_x.shape

    def body(mid_ref, before_ref, after_ref, tiles_ref, label_ref, out_ref, low_ref, high_ref, cat_ref):
        cat_ref[:BAND] = before_ref[0]
        cat_ref[BAND : BAND + slab_x] = mid_ref[0]
        cat_ref[BAND + slab_x :] = after_ref[0]
        label = label_ref[0]
        for t in range(tiles):
            columns = cat_ref[t * rows : t * rows + window]
            total = jnp.dot(tiles_ref[0, t], columns, preferred_element_type=jnp.float32)
            for level in range(1, classes):
                product = jnp.dot(tiles_ref[level, t], columns, preferred_element_type=jnp.float32)
                total = jnp.where(label == level, product, total)
            bounded = (soft_bound * jnp.tanh(total / soft_bound)).astype(jnp.bfloat16)
            out_ref[0, t * rows : (t + 1) * rows] = bounded
            low_ref[0, t * rows : (t + 1) * rows] = bounded[:, :BAND]
            high_ref[0, t * rows : (t + 1) * rows] = bounded[:, wide - BAND :]

    full = pl.BlockSpec((1, slab_x, wide), lambda m: (m, 0, 0))
    edge = pl.BlockSpec((1, BAND, wide), lambda m: (m, 0, 0))
    side = pl.BlockSpec((1, slab_x, BAND), lambda m: (m, 0, 0))
    size = slots * slab_x * wide
    return pl.pallas_call(
        body,
        grid=(slots,),
        in_specs=[
            full,
            edge,
            edge,
            pl.BlockSpec(tiles_x.shape, lambda m: (0, 0, 0, 0)),
            pl.BlockSpec((1, 1, wide), lambda m: (first + m, 0, 0)),
        ],
        out_specs=[full, side, side],
        out_shape=[
            jax.ShapeDtypeStruct((slots, slab_x, wide), jnp.bfloat16),
            jax.ShapeDtypeStruct((slots, slab_x, BAND), jnp.bfloat16),
            jax.ShapeDtypeStruct((slots, slab_x, BAND), jnp.bfloat16),
        ],
        scratch_shapes=[pltpu.VMEM((slab_x + 2 * BAND, wide), jnp.bfloat16)],
        compiler_params=params(),
        cost_estimate=cost(2 * classes * window * size, 6 * size, size),
        name="smooth_x",
    )(scaled, before, after, tiles_x, labels)


def smooth_y(bounded, before, after, tiles_y, labels, place, first):
    slots, slab_x, wide = bounded.shape
    classes, tiles, window, narrow = tiles_y.shape

    def body(place_ref, mid_ref, before_ref, after_ref, tiles_ref, label_ref, keep_ref, send_ref, cat_ref):
        cat_ref[:, :BAND] = before_ref[0]
        cat_ref[:, BAND : BAND + wide] = mid_ref[0]
        cat_ref[:, BAND + wide :] = after_ref[0]
        label = label_ref[0]
        left = place_ref[0] == 0
        halves = []
        for t in range(tiles):
            columns = cat_ref[:, t * narrow : t * narrow + window]
            total = jnp.dot(columns, tiles_ref[0, t], preferred_element_type=jnp.float32)
            for level in range(1, classes):
                product = jnp.dot(columns, tiles_ref[level, t], preferred_element_type=jnp.float32)
                total = jnp.where(label == level, product, total)
            halves.append(total.astype(jnp.bfloat16))
        keep_ref[0] = jnp.where(left, halves[0], halves[1])
        send_ref[0] = jnp.where(left, halves[1], halves[0])

    full = pl.BlockSpec((1, slab_x, wide), lambda m, place_ref: (m, 0, 0))
    side = pl.BlockSpec((1, slab_x, BAND), lambda m, place_ref: (m, 0, 0))
    block = pl.BlockSpec((1, slab_x, narrow), lambda m, place_ref: (m, 0, 0))
    size = slots * slab_x * wide
    out = jax.ShapeDtypeStruct((slots, slab_x, narrow), jnp.bfloat16)
    return pl.pallas_call(
        body,
        grid_spec=pltpu.PrefetchScalarGridSpec(
            num_scalar_prefetch=1,
            grid=(slots,),
            in_specs=[
                full,
                side,
                side,
                pl.BlockSpec(tiles_y.shape, lambda m, place_ref: (0, 0, 0, 0)),
                pl.BlockSpec((1, slab_x, 1), lambda m, place_ref: (first + m, 0, 0)),
            ],
            out_specs=[block, block],
            scratch_shapes=[pltpu.VMEM((slab_x, wide + 2 * BAND), jnp.bfloat16)],
        ),
        out_shape=[out, out],
        compiler_params=params(),
        cost_estimate=cost(2 * classes * window * size, 6 * size),
        name="smooth_y",
    )(place, bounded, before, after, tiles_y, labels)


def join_planes(kept, came, perm_back, slots_of, planes, rows):
    _, slab_x, narrow = kept[0].shape
    span = perm_back.shape[0]
    sub = span // planes
    half = planes // PAIR
    kernels = len(slots_of) // half
    count = len(kept)

    def body(*refs):
        kept_refs, came_refs = refs[:count], refs[count : 2 * count]
        perm_ref, out_ref, stack_ref = refs[2 * count :]
        for k in range(kernels):
            for b in range(rows // sub):
                for j in range(half):
                    c, m = slots_of[k * half + j]
                    at = slice(b * sub, (b + 1) * sub)
                    stack_ref[j * sub : (j + 1) * sub] = kept_refs[c][m, at]
                    stack_ref[(half + j) * sub : (half + j + 1) * sub] = came_refs[c][m, at]
                moved = jnp.dot(perm_ref[...], stack_ref[...], preferred_element_type=jnp.float32)
                moved = moved.reshape(sub, planes, narrow).astype(jnp.bfloat16)
                out_ref[b * sub : (b + 1) * sub, k] = moved

    specs = [pl.BlockSpec((a.shape[0], rows, narrow), lambda i: (0, i, 0)) for a in kept]
    size = slab_x * kernels * planes * narrow
    return pl.pallas_call(
        body,
        grid=(slab_x // rows,),
        in_specs=specs + specs + [pl.BlockSpec(perm_back.shape, lambda i: (0, 0))],
        out_specs=pl.BlockSpec((rows, kernels, planes, narrow), lambda i: (i, 0, 0, 0)),
        out_shape=jax.ShapeDtypeStruct((slab_x, kernels, planes, narrow), jnp.bfloat16),
        scratch_shapes=[pltpu.VMEM((span, narrow), jnp.bfloat16)],
        compiler_params=params(),
        cost_estimate=cost(2 * span * size, 4 * size),
        name="join_planes",
    )(*kept, *came, perm_back)


def per_device(partial_kernels, illumination, classes_x, classes_y, widths_x, widths_y):
    _, slab_x, kernels, planes, full_y = partial_kernels.shape
    groups = lax.axis_size("ev")
    owners = lax.axis_size("gx")
    slab_y = full_y // groups
    full_x = slab_x * owners
    shards = groups // PAIR
    half = planes // PAIR
    me = lax.axis_index("ev")
    pair = lax.rem(me, PAIR)
    line = me // PAIR
    place = pair.astype(jnp.int32).reshape(1)

    other = [(i, i ^ 1) for i in range(groups)]
    z_up = [(i, i + PAIR) for i in range(groups - PAIR)]
    z_down = [(b, a) for a, b in z_up]
    x_up = [(i, i + 1) for i in range(owners - 1)]
    x_down = [(b, a) for a, b in x_up]
    lines = [[z * PAIR + y for z in range(shards)] for y in range(PAIR)]

    def over_line(parts):
        return lax.psum_scatter(
            parts, "ev", scatter_dimension=0, axis_index_groups=lines, tiled=True
        ).reshape(parts.shape[1:])

    sub = 256 // planes
    span = sub * planes
    to_row = lax.broadcasted_iota(jnp.int32, (span, span), 0)
    from_row = lax.broadcasted_iota(jnp.int32, (span, span), 1)
    plane_of = lax.rem(to_row // sub + half * pair, planes)
    perm = (from_row == lax.rem(to_row, sub) * planes + plane_of).astype(jnp.bfloat16)
    chunks = plan_chunks(kernels, half)

    lit_planes = jnp.transpose(illumination, (1, 0, 2))
    lit = lax.dynamic_slice_in_dim(lit_planes, half * pair, half, 0)
    lit_sent = lax.dynamic_slice_in_dim(lit_planes, half * (1 - pair), half, 0).astype(jnp.bfloat16)
    lit_pair = lax.ppermute(lit_sent, "ev", other)

    split, before = {}, []
    for some in (chunks[:1], chunks[1:2], chunks[2:]):
        for k in range(kernels):
            mine = [c for c in some if c[1] == k]
            if mine:
                arrays = list(split_planes(partial_kernels, perm, k, mine, shards, slab_x, before))
                before = arrays[:1]
                for c in mine:
                    split[c] = (arrays.pop(0),) if c[0] == "zy" else (arrays.pop(0), arrays.pop(0))

    labels_mine = lax.dynamic_slice_in_dim(classes_x, half * pair, half, 0)
    labels_sent = lax.dynamic_slice_in_dim(classes_x, half * (1 - pair), half, 0)
    labels_pair = lax.ppermute(labels_sent, "ev", other)
    labels_x = jnp.where(
        pair == 0,
        jnp.concatenate([labels_mine, labels_pair], 1),
        jnp.concatenate([labels_pair, labels_mine], 1),
    ).reshape(half, 1, PAIR * slab_y)
    labels_y = lax.dynamic_slice_in_dim(classes_y.T, half * pair, half, 0).reshape(half, slab_x, 1)

    tile = min(256, slab_x)
    tiles_x = band_tiles(full_x, widths_x, lax.axis_index("gx") * slab_x, slab_x // tile, tile)
    tiles_y = jnp.swapaxes(band_tiles(full_y, widths_y, line * PAIR * slab_y, PAIR, slab_y), 2, 3)

    own, sent = split[chunks[1]]
    split[chunks[1]] = own, hold(sent, [lit_pair, split[chunks[2]][0]])

    slots_of, sums, kept, came = {}, {}, {}, {}
    for n, (order, k, first, slots) in enumerate(chunks):
        for m in range(slots):
            slots_of[k * half + first + m] = (n, m)

    def begin(n, after=()):
        order, k, first, slots = chunks[n]
        if order == "yz":
            own, sent = split[chunks[n]]
            sums[n] = [over_line(add_parts(own, lax.ppermute(sent, "ev", other), after))]
        else:
            both = over_line(split[chunks[n]][0])
            sums[n] = [both[:slots], lax.ppermute(both[slots:], "ev", other)]

    def finish(n, after=()):
        order, k, first, slots = chunks[n]
        scaled, top, bottom = scale(sums[n], lit, lit_pair, place, first, after)
        before = lax.ppermute(bottom, "gx", x_up)
        after = lax.ppermute(top, "gx", x_down)
        bounded, low, high = smooth_x(scaled, before, after, tiles_x, labels_x, first)
        before = lax.ppermute(high, "ev", z_up)
        after = lax.ppermute(low, "ev", z_down)
        kept[n], send = smooth_y(bounded, before, after, tiles_y, labels_y, place, first)
        came[n] = lax.ppermute(send, "ev", other)

    last = len(chunks)
    begin(0)
    begin(1)
    begin(2, [sums[0][1]])
    finish(1)
    begin(3, [kept[1]])
    finish(0)
    for n in range(4, last):
        begin(n, [kept[0]])
    finish(2, [kept[0], came[1]])
    for n in range(3, last):
        finish(n, [came[0]])
    order = range(last)
    return join_planes([kept[n] for n in order], [came[n] for n in order], perm.T, slots_of, planes, slab_x // 2)


def solution(mesh):
    return jax.shard_map(
        per_device,
        mesh=mesh,
        in_specs=(
            P("ev", "gx", None, None, None),
            P("gx", None, "ev"),
            P(None, "ev"),
            P("gx", None),
            P(),
            P(),
        ),
        out_specs=P("gx", None, None, "ev"),
        check_vma=False,
    )
```

time: 729 us -> 509 us (0.70)
  waiting for transfers between devices: 623 us -> 281 us
  Pallas kernels: 0 us -> 120 us
  starting transfers between devices: 11.1 us -> 57.7 us
  matrix products: 42.1 us -> 0 us
    reduce_scatter x1 -> x5, waiting for transfers between devices: 547 us -> 23.9 us  [over_line(): lax.psum_scatter(parts, 'ev', scatter_dimension=0, axis_index_groups=line...]
    ppermute x4 -> x32, waiting for transfers between devices: 75.6 us -> 257 us  [the longest x4 161 us: begin(): lax.ppermute(sent, 'ev', other)]
    pallas_call x0 -> x24, Pallas kernels: none -> 120 us  [the longest x3 35.5 us: split_planes(): pl.pallas_call(body, grid=(shards, slab_x // rows), in_specs=[pl.BlockSpe...]
    ppermute x4 -> x32, starting transfers between devices: 11.1 us -> 57.5 us  [the longest x5 17.5 us: finish(): before = lax.ppermute(bottom, 'gx', x_up)]
    dot_general x6 -> x0, matrix products: 42.1 us -> none  [the longest x3 23.5 us: smooth_columns(): jnp.dot(matrices[level], columns, preferred_element_type=jnp.float32)]
    unnamed x14 -> x72, local copies, waits for them, and re-layouts: 6.22 us -> 16.8 us
    concatenate x1 -> x2, local copies, waits for them, and re-layouts: 7.64 us -> 0.01 us  [per_device(): jnp.concatenate([labels_mine, labels_pair], 1)]
  transfers between devices with their start and end apart: 5 -> 37, of which waited for: 4 -> 19; matrix products, arithmetic and copies ran while one was open for 2% -> 4% of each run, Pallas kernels for 0% -> 21%
where the time goes in v1:
time: 509 us; the launch traced here: 507 us
  waiting for transfers between devices  281 us (55%)
  Pallas kernels  120 us (24%)
  starting transfers between devices  57.7 us (11%)
  local copies, waits for them, and re-layouts  26.1 us (5%)
  between operations  13.6 us (3%)
  other arithmetic  8.75 us (2%)
    ppermute x4, waiting for transfers between devices, begin(): lax.ppermute(sent, 'ev', other)  161 us
    pallas_call x3, Pallas kernels, split_planes(): pl.pallas_call(body, grid=(shards, slab_x // rows), in_specs=[pl.BlockSpe...  35.5 us
    pallas_call x4, Pallas kernels, add_parts(): pl.pallas_call(body, grid=(shards, slots), in_specs=[spec, spec] + [pl.Bl...  24.4 us
    ppermute x5, waiting for transfers between devices, finish(): after = lax.ppermute(low, 'ev', z_down)  24 us
    reduce_scatter x5, waiting for transfers between devices, over_line(): lax.psum_scatter(parts, 'ev', scatter_dimension=0, axis_index_groups=line...  23.9 us
    ppermute x1, waiting for transfers between devices, begin(): sums[n] = [both[:slots], lax.ppermute(both[slots:], 'ev', other)]  22.4 us
    pallas_call x5, Pallas kernels, smooth_x(): pl.pallas_call(body, grid=(slots,), in_specs=[full, edge, edge, pl.BlockS...  21.9 us
    pallas_call x5, Pallas kernels, smooth_y(): pl.pallas_call(body, grid_spec=pltpu.PrefetchScalarGridSpec(num_scalar_pr...  20.9 us
  transfers between devices with their start and end apart: 37, of which 19 were waited for; matrix products, arithmetic and copies ran while one was open for 4% of the time, Pallas kernels for 21%

profile of v1, /device:TPU:1, one launch (start us, length us, event | category | flops | bytes accessed | tf_op | source)
XLA Modules:
  0.0 507.3 jit_solution(11149125634784950882)
XLA Ops:
  7.5 11.1 %split_planes.3.refs_0_ = bf16[4,4,512,512]{3,2,1,0:T(8,128)(2,1)} custom-call(bf16[1,512,2,8,2048]{4,3,2,1,0:T(8,128)(2,1)} %part_ref.5, bf16[256,256]{1,0:T(8,128)(2,1)} %get-tuple-element.106.perm_ref), custom_call_target="tpu_custom_call" | custom-call | tf_op jit(solution)/shard_map/split_planes/pallas_call | solution.py:63
  18.6 2.6 constant_dynamic-slice_fusion.2
  23.5 11.1 %split_planes.4 = (bf16[4,2,512,512]{3,2,1,0:T(8,128)(2,1)}, bf16[4,2,512,512]{3,2,1,0:T(8,128)(2,1)}) custom-call(bf16[1,512,2,8,2048]{4,3,2,1,0:T(8,128)(2,1)} %part_ref.5, bf16[256,256]{1,0:T(8,128)(2,1)} %get-tuple-element.106.perm_ref, bf16[4,4,512,512]{3,2,1,0:T(8,128)(2,1)} %split_planes.3.refs_0_), custom_call_target="tpu_custom_call" | custom-call | tf_op jit(solution)/shard_map/split_planes/pallas_call | solution.py:63
  34.6 13.3 %split_planes.5 = (bf16[4,2,512,512]{3,2,1,0:T(8,128)(2,1)}, bf16[4,2,512,512]{3,2,1,0:T(8,128)(2,1)}, bf16[4,1,512,512]{3,2,1,0:T(8,128)(2,1)}, bf16[4,1,512,51...) custom-call(bf16[1,512,2,8,2048]{4,3,2,1,0:T(8,128)(2,1)} %part_ref.5, ...), custom_call_target="tpu_custom_call" | custom-call | tf_op jit(solution)/shard_map/split_planes/pallas_call | solution.py:63
  49.1 91.3 %collective-permute-done.7.b_ref = bf16[4,2,512,512]{3,2,1,0:T(8,128)(2,1)} collective-permute-done((bf16[4,2,512,512]{3,2,1,0:T(8,128)(2,1)}, bf16[4,2,512,512]{3,2,1,0:T(8,128)(2,1)}, u32[]{:S(2)}, u32[]{:S(2)}) %collective-permute-start.7) | collective-permute-done | bytes 4194336 | tf_op jit(solution)/shard_map/ppermute | solution.py:378
  140.3 7.8 %add_parts.4 = bf16[4,2,512,512]{3,2,1,0:T(8,128)(2,1)} custom-call(bf16[4,2,512,512]{3,2,1,0:T(8,128)(2,1)} %get-tuple-element.60.refs_0_.a_ref, bf16[4,2,512,512]{3,2,1,0:T(8,128)(2,1)} %collective-permute-done.7.b_ref), custom_call_target="tpu_custom_call" | custom-call | flops 2097152 | bytes 12582912 | tf_op jit(solution)/shard_map/add_parts/pallas_call | solution.py:104
  148.4 16.8 %reduce-scatter.6.cloned.1.call-done = bf16[1,4,512,512]{3,2,1,0:T(8,128)(2,1)} async-done(((bf16[4,4,512,512]{3,2,1,0:T(8,128)(2,1)}), bf16[1,4,512,512]{3,2,1,0:T(8,128)(2,1)}) %reduce-scatter.6.cloned.1.call-update) | async-done | bytes 2097168 | tf_op jit(solution)/shard_map/reduce_scatter | solution.py:325
  165.1 2.8 slice_bitcast_fusion
  169.1 69.8 %collective-permute-done.12.b_ref = bf16[4,2,512,512]{3,2,1,0:T(8,128)(2,1)} collective-permute-done((bf16[4,2,512,512]{3,2,1,0:T(8,128)(2,1)}, bf16[4,2,512,512]{3,2,1,0:T(8,128)(2,1)}, u32[]{:S(2)}, u32[]{:S(2)}) %collective-permute-start.12) | collective-permute-done | bytes 4194336 | tf_op jit(solution)/shard_map/ppermute | solution.py:378
  238.8 22.4 %collective-permute-done.refs_1_.refs_0_ = bf16[2,512,512]{2,1,0:T(8,128)(2,1)S(1)} collective-permute-done((bf16[2,512,512]{2,1,0:T(8,128)(2,1)S(1)}, bf16[2,512,512]{2,1,0:T(8,128)(2,1)S(1)}, u32[]{:S(2)}, u32[]{:S(2)}) %collective-permute-start) | collective-permute-done | bytes 1048608 | tf_op jit(solution)/shard_map/ppermute | solution.py:381
  262.3 7.8 %add_parts.5 = bf16[4,2,512,512]{3,2,1,0:T(8,128)(2,1)} custom-call(bf16[4,2,512,512]{3,2,1,0:T(8,128)(2,1)} %get-tuple-element.62.refs_2_.a_ref, bf16[4,2,512,512]{3,2,1,0:T(8,128)(2,1)} %collective-permute-done.12.b_ref, bf16[2,512,512]{2,1,0:T(8,128)(2,1)} %copy-done.3), custom_call_target="tpu_custom_call" | custom-call | flops 2097152 | bytes 12582912 | tf_op jit(solution)/shard_map/add_parts/pallas_call | solution.py:104
  272.3 2.5 constant_dynamic-slice_fusion.3
  276.6 3.2 add_convert_fusion.tiles_ref
  279.8 2.8 scale.6
  282.6 6.3 %collective-permute-start.8 = (bf16[2,128,512]{2,1,0:T(8,128)(2,1)}, bf16[2,128,512]{2,1,0:T(8,128)(2,1)S(1)}, u32[]{:S(2)}, u32[]{:S(2)}) collective-permute-start(bf16[2,128,512]{2,1,0:T(8,128)(2,1)} %get-tuple-element.64), channel_id=1, source_target_pairs={{0,8},{8,16},{16,24},{1,9},{9,17},{17,25},{2,10},{10,18},{18,26},{... | collective-permute-start | bytes 786440 | tf_op jit(solution)/shard_map/ppermute | solution.py:386
  293.1 4.1 collective-permute-done.9.after_ref
  297.9 5.0 smooth_x.6
  302.9 3.1 collective-permute-start.10
  307.5 2.5 fusion.16.tiles_ref
  311.4 5.5 %collective-permute-done.10.before_ref = bf16[2,512,128]{2,1,0:T(8,128)(2,1)S(1)} collective-permute-done((bf16[2,512,128]{2,1,0:T(8,128)(2,1)}, bf16[2,512,128]{2,1,0:T(8,128)(2,1)S(1)}, u32[]{:S(2)}, u32[]{:S(2)}) %collective-permute-start.10) | collective-permute-done | bytes 262176 | tf_op jit(solution)/shard_map/ppermute | solution.py:389
  316.9 10.4 %collective-permute-done.11.after_ref = bf16[2,512,128]{2,1,0:T(8,128)(2,1)S(1)} collective-permute-done((bf16[2,512,128]{2,1,0:T(8,128)(2,1)}, bf16[2,512,128]{2,1,0:T(8,128)(2,1)S(1)}, u32[]{:S(2)}, u32[]{:S(2)}) %collective-permute-start.11) | collective-permute-done | bytes 262176 | tf_op jit(solution)/shard_map/ppermute | solution.py:390
  327.9 4.6 smooth_y.6
  333.9 4.3 add_parts.6
  338.9 3.1 scale.5
  342.1 2.8 collective-permute-start.2
  348.5 4.7 collective-permute-done.3.after_ref
  353.9 4.9 smooth_x.5
  358.8 3.1 collective-permute-start.5
  363.2 5.2 %collective-permute-done.5.before_ref = bf16[2,512,128]{2,1,0:T(8,128)(2,1)S(1)} collective-permute-done((bf16[2,512,128]{2,1,0:T(8,128)(2,1)}, bf16[2,512,128]{2,1,0:T(8,128)(2,1)S(1)}, u32[]{:S(2)}, u32[]{:S(2)}) %collective-permute-start.5) | collective-permute-done | bytes 262176 | tf_op jit(solution)/shard_map/ppermute | solution.py:389
  368.4 12.1 %collective-permute-done.6.after_ref = bf16[2,512,128]{2,1,0:T(8,128)(2,1)S(1)} collective-permute-done((bf16[2,512,128]{2,1,0:T(8,128)(2,1)}, bf16[2,512,128]{2,1,0:T(8,128)(2,1)S(1)}, u32[]{:S(2)}, u32[]{:S(2)}) %collective-permute-start.6) | collective-permute-done | bytes 262176 | tf_op jit(solution)/shard_map/ppermute | solution.py:390
  381.2 4.7 smooth_y.5
  387.2 4.4 add_parts.7
  391.7 2.4 collective-permute-start.13
  394.2 9.7 %collective-permute-done.13.refs_4_.refs_6_ = bf16[2,512,256]{2,1,0:T(8,128)(2,1)S(1)} collective-permute-done((bf16[2,512,256]{2,1,0:T(8,128)(2,1)S(1)}, bf16[2,512,256]{2,1,0:T(8,128)(2,1)S(1)}, u32[]{:S(2)}, u32[]{:S(2)}) %collective-permute-start.13) | collective-permute-done | bytes 524320 | tf_op jit(solution)/shard_map/ppermute | solution.py:392
  404.8 2.7 scale.7
  413.1 4.7 collective-permute-done.15.after_ref
  418.5 4.9 smooth_x.7
  433.5 4.5 collective-permute-done.21.after_ref
  438.6 3.6 smooth_x.8
  442.2 4.0 collective-permute-start.22
  447.4 7.1 %reduce-scatter.14.cloned.1.call-done = bf16[1,1,512,512]{3,2,1,0:T(8,128)(2,1)} async-done(((bf16[4,1,512,512]{3,2,1,0:T(8,128)(2,1)}), bf16[1,1,512,512]{3,2,1,0:T(8,128)(2,1)}) %reduce-scatter.14.cloned.1.call-update) | async-done | bytes 524304 | tf_op jit(solution)/shard_map/reduce_scatter | solution.py:325
  456.9 4.5 collective-permute-start.25
  464.1 4.6 smooth_y.7
  470.6 3.5 smooth_x.9
  477.7 3.5 smooth_y.8
  483.6 3.5 smooth_y.9
  487.6 7.8 %collective-permute-done.31.refs_9_ = bf16[1,512,256]{2,1,0:T(8,128)(2,1)S(1)} collective-permute-done((bf16[1,512,256]{2,1,0:T(8,128)(2,1)}, bf16[1,512,256]{2,1,0:T(8,128)(2,1)S(1)}, u32[]{:S(2)}, u32[]{:S(2)}) %collective-permute-start.31) | collective-permute-done | bytes 262176 | tf_op jit(solution)/shard_map/ppermute | solution.py:392
  496.4 4.4 join_planes.1
  (147 shorter events, 62.1 us)
Async XLA Ops:
  6.5 303.5 %copy-start = (s32[512,8]{0,1:T(8,128)S(1)}, s32[512,8]{0,1:T(8,128)}, u32[]{:S(2)}) copy-start(s32[512,8]{0,1:T(8,128)} %param.9) | copy-start | bytes 49156
  6.5 158.6 %reduce-scatter.6.cloned.1.call-start = ((), (), s32[]{:S(2)}) async-start(), calls=%async_computation.5 | async-start | bytes 10485760 | tf_op jit(solution)/shard_map/reduce_scatter | solution.py:325
  18.6 261.2 %reduce-scatter.8.cloned.1.call-start = ((), (), s32[]{:S(2)}) async-start(), calls=%async_computation.6 | async-start | bytes 5242880 | tf_op jit(solution)/shard_map/reduce_scatter | solution.py:325
  21.4 26.5 %collective-permute-start.1 = (bf16[4,512,256]{2,1,0:T(8,128)(2,1)S(1)}, bf16[4,512,256]{2,1,0:T(8,128)(2,1)S(1)}, u32[]{:S(2)}, u32[]{:S(2)}) collective-permute-start(bf16[4,512,256]{2,1,0:T(8,128)(2,1)S(1)} %bitcast.25), channel_id=1, source_target_pairs={{0,1},{1,0},{2,3},{3,2},{4,5},{5,4},{6,7},{7,6},{8,9},{9,8},{10,11... | collective-permute-start | bytes 3145736 | tf_op jit(solution)/shard_map/ppermute | solution.py:340
  48.9 91.4 %collective-permute-start.7 = (bf16[4,2,512,512]{3,2,1,0:T(8,128)(2,1)}, bf16[4,2,512,512]{3,2,1,0:T(8,128)(2,1)}, u32[]{:S(2)}, u32[]{:S(2)}) collective-permute-start(bf16[4,2,512,512]{3,2,1,0:T(8,128)(2,1)} %hold.1), channel_id=1, source_target_pairs={{0,1},{1,0},{2,3},{3,2},{4,5},{5,4},{6,7},{7,6},{8,9},{9,8},{10,11... | collective-permute-start | bytes 12582920 | tf_op jit(solution)/shard_map/ppermute | solution.py:378
  148.2 255.8 %reduce-scatter.10.cloned.1.call-start = ((), (), s32[]{:S(2)}) async-start(), calls=%async_computation.7 | async-start | bytes 5242880 | tf_op jit(solution)/shard_map/reduce_scatter | solution.py:325
  148.3 90.6 %collective-permute-start.12 = (bf16[4,2,512,512]{3,2,1,0:T(8,128)(2,1)}, bf16[4,2,512,512]{3,2,1,0:T(8,128)(2,1)}, u32[]{:S(2)}, u32[]{:S(2)}) collective-permute-start(bf16[4,2,512,512]{3,2,1,0:T(8,128)(2,1)} %get-tuple-element.70), channel_id=1, source_target_pairs={{0,1},{1,0},{2,3},{3,2},{4,5},{5,4},{6,7},{7,6},{8,9},{9,8},{10,11... | collective-permute-start | bytes 12582920 | tf_op jit(solution)/shard_map/ppermute | solution.py:378
  167.9 93.3 %collective-permute-start = (bf16[2,512,512]{2,1,0:T(8,128)(2,1)S(1)}, bf16[2,512,512]{2,1,0:T(8,128)(2,1)S(1)}, u32[]{:S(2)}, u32[]{:S(2)}) collective-permute-start(bf16[2,512,512]{2,1,0:T(8,128)(2,1)S(1)} %get-tuple-element.101), channel_id=1, source_target_pairs={{0,1},{1,0},{2,3},{3,2},{4,5},{5,4},{6,7},{7,6},{8,9},{9,8},{10,11... | collective-permute-start | bytes 3145736 | tf_op jit(solution)/shard_map/ppermute | solution.py:381
  270.1 155.8 %reduce-scatter.12.cloned.1.call-start = ((), (), s32[]{:S(2)}) async-start(), calls=%async_computation.8 | async-start | bytes 2621440 | tf_op jit(solution)/shard_map/reduce_scatter | solution.py:325
  270.8 21.6 %collective-permute-start.4 = (s32[4,256]{1,0:T(4,128)S(1)}, s32[4,256]{1,0:T(4,128)S(1)}, u32[]{:S(2)}, u32[]{:S(2)}) collective-permute-start(s32[4,256]{1,0:T(4,128)S(1)} %get-tuple-element.104), channel_id=1, source_target_pairs={{0,1},{1,0},{2,3},{3,2},{4,5},{5,4},{6,7},{7,6},{8,9},{9,8},{10,11... | collective-permute-start | bytes 12296 | tf_op jit(solution)/shard_map/ppermute | solution.py:354
  270.8 61.7 %collective-permute-start.18 = (bf16[4,1,512,512]{3,2,1,0:T(8,128)(2,1)}, bf16[4,1,512,512]{3,2,1,0:T(8,128)(2,1)S(1)}, u32[]{:S(2)}, u32[]{:S(2)}) collective-permute-start(bf16[4,1,512,512]{3,2,1,0:T(8,128)(2,1)} %get-tuple-element.80), channel_id=1, source_target_pairs={{0,1},{1,0},{2,3},{3,2},{4,5},{5,4},{6,7},{7,6},{8,9},{9,8},{10,11... | collective-permute-start | bytes 6291464 | tf_op jit(solution)/shard_map/ppermute | solution.py:378
  282.6 10.5 %collective-permute-start.8 = (bf16[2,128,512]{2,1,0:T(8,128)(2,1)}, bf16[2,128,512]{2,1,0:T(8,128)(2,1)S(1)}, u32[]{:S(2)}, u32[]{:S(2)}) collective-permute-start(bf16[2,128,512]{2,1,0:T(8,128)(2,1)} %get-tuple-element.64), channel_id=1, source_target_pairs={{0,8},{8,16},{16,24},{1,9},{9,17},{17,25},{2,10},{10,18},{18,26},{... | collective-permute-start | bytes 786440 | tf_op jit(solution)/shard_map/ppermute | solution.py:386
  288.9 8.3 %collective-permute-start.9 = (bf16[2,128,512]{2,1,0:T(8,128)(2,1)}, bf16[2,128,512]{2,1,0:T(8,128)(2,1)S(1)}, u32[]{:S(2)}, u32[]{:S(2)}) collective-permute-start(bf16[2,128,512]{2,1,0:T(8,128)(2,1)} %get-tuple-element.65), channel_id=1, source_target_pairs={{8,0},{16,8},{24,16},{9,1},{17,9},{25,17},{10,2},{18,10},{26,18},{... | collective-permute-start | bytes 786440 | tf_op jit(solution)/shard_map/ppermute | solution.py:387
  293.1 4.1 copy-start.19
  302.9 13.9 %collective-permute-start.10 = (bf16[2,512,128]{2,1,0:T(8,128)(2,1)}, bf16[2,512,128]{2,1,0:T(8,128)(2,1)S(1)}, u32[]{:S(2)}, u32[]{:S(2)}) collective-permute-start(bf16[2,512,128]{2,1,0:T(8,128)(2,1)} %get-tuple-element.67), channel_id=1, source_target_pairs={{0,2},{1,3},{2,4},{3,5},{4,6},{5,7},{8,10},{9,11},{10,12},{11,13},... | collective-permute-start | bytes 786440 | tf_op jit(solution)/shard_map/ppermute | solution.py:389
  306.1 21.2 %collective-permute-start.11 = (bf16[2,512,128]{2,1,0:T(8,128)(2,1)}, bf16[2,512,128]{2,1,0:T(8,128)(2,1)S(1)}, u32[]{:S(2)}, u32[]{:S(2)}) collective-permute-start(bf16[2,512,128]{2,1,0:T(8,128)(2,1)} %get-tuple-element.68), channel_id=1, source_target_pairs={{2,0},{3,1},{4,2},{5,3},{6,4},{7,5},{10,8},{11,9},{12,10},{13,11},... | collective-permute-start | bytes 786440 | tf_op jit(solution)/shard_map/ppermute | solution.py:390
  316.9 10.4 %copy-start.21 = (bf16[2,512,128]{2,1,0:T(8,128)(2,1)}, bf16[2,512,128]{2,1,0:T(8,128)(2,1)S(1)}, u32[]{:S(2)}) copy-start(bf16[2,512,128]{2,1,0:T(8,128)(2,1)S(1)} %collective-permute-done.10.before_ref) | copy-start | bytes 786436
  338.2 116.3 %reduce-scatter.14.cloned.1.call-start = ((), (), s32[]{:S(2)}) async-start(), calls=%async_computation.9 | async-start | bytes 2621440 | tf_op jit(solution)/shard_map/reduce_scatter | solution.py:325
  338.3 47.5 %collective-permute-start.24 = (bf16[4,1,512,512]{3,2,1,0:T(8,128)(2,1)}, bf16[4,1,512,512]{3,2,1,0:T(8,128)(2,1)S(1)}, u32[]{:S(2)}, u32[]{:S(2)}) collective-permute-start(bf16[4,1,512,512]{3,2,1,0:T(8,128)(2,1)} %get-tuple-element.90), channel_id=1, source_target_pairs={{0,1},{1,0},{2,3},{3,2},{4,5},{5,4},{6,7},{7,6},{8,9},{9,8},{10,11... | collective-permute-start | bytes 6291464 | tf_op jit(solution)/shard_map/ppermute | solution.py:378
  342.1 6.4 %collective-permute-start.2 = (bf16[2,128,512]{2,1,0:T(8,128)(2,1)}, bf16[2,128,512]{2,1,0:T(8,128)(2,1)S(1)}, u32[]{:S(2)}, u32[]{:S(2)}) collective-permute-start(bf16[2,128,512]{2,1,0:T(8,128)(2,1)} %get-tuple-element.54), channel_id=1, source_target_pairs={{0,8},{8,16},{16,24},{1,9},{9,17},{17,25},{2,10},{10,18},{18,26},{... | collective-permute-start | bytes 786440 | tf_op jit(solution)/shard_map/ppermute | solution.py:386
  344.9 8.3 %collective-permute-start.3 = (bf16[2,128,512]{2,1,0:T(8,128)(2,1)}, bf16[2,128,512]{2,1,0:T(8,128)(2,1)S(1)}, u32[]{:S(2)}, u32[]{:S(2)}) collective-permute-start(bf16[2,128,512]{2,1,0:T(8,128)(2,1)} %get-tuple-element.55), channel_id=1, source_target_pairs={{8,0},{16,8},{24,16},{9,1},{17,9},{25,17},{10,2},{18,10},{26,18},{... | collective-permute-start | bytes 786440 | tf_op jit(solution)/shard_map/ppermute | solution.py:387
  348.5 4.7 copy-start.23
  358.8 9.6 %collective-permute-start.5 = (bf16[2,512,128]{2,1,0:T(8,128)(2,1)}, bf16[2,512,128]{2,1,0:T(8,128)(2,1)S(1)}, u32[]{:S(2)}, u32[]{:S(2)}) collective-permute-start(bf16[2,512,128]{2,1,0:T(8,128)(2,1)} %get-tuple-element.57), channel_id=1, source_target_pairs={{0,2},{1,3},{2,4},{3,5},{4,6},{5,7},{8,10},{9,11},{10,12},{11,13},... | collective-permute-start | bytes 786440 | tf_op jit(solution)/shard_map/ppermute | solution.py:389
  361.9 18.6 %collective-permute-start.6 = (bf16[2,512,128]{2,1,0:T(8,128)(2,1)}, bf16[2,512,128]{2,1,0:T(8,128)(2,1)S(1)}, u32[]{:S(2)}, u32[]{:S(2)}) collective-permute-start(bf16[2,512,128]{2,1,0:T(8,128)(2,1)} %get-tuple-element.58), channel_id=1, source_target_pairs={{2,0},{3,1},{4,2},{5,3},{6,4},{7,5},{10,8},{11,9},{12,10},{13,11},... | collective-permute-start | bytes 786440 | tf_op jit(solution)/shard_map/ppermute | solution.py:390
  368.4 12.1 %copy-start.25 = (bf16[2,512,128]{2,1,0:T(8,128)(2,1)}, bf16[2,512,128]{2,1,0:T(8,128)(2,1)S(1)}, u32[]{:S(2)}) copy-start(bf16[2,512,128]{2,1,0:T(8,128)(2,1)S(1)} %collective-permute-done.5.before_ref) | copy-start | bytes 786436
  387.2 4.5 copy-start.15
  387.2 6.9 %copy-start.16 = (bf16[2,512,256]{2,1,0:T(8,128)(2,1)S(1)}, bf16[2,512,256]{2,1,0:T(8,128)(2,1)}, u32[]{:S(2)}) copy-start(bf16[2,512,256]{2,1,0:T(8,128)(2,1)} %get-tuple-element.81) | copy-start | bytes 1572868
  391.7 12.3 %collective-permute-start.13 = (bf16[2,512,256]{2,1,0:T(8,128)(2,1)S(1)}, bf16[2,512,256]{2,1,0:T(8,128)(2,1)S(1)}, u32[]{:S(2)}, u32[]{:S(2)}) collective-permute-start(bf16[2,512,256]{2,1,0:T(8,128)(2,1)S(1)} %copy-done.15), channel_id=1, source_target_pairs={{0,1},{1,0},{2,3},{3,2},{4,5},{5,4},{6,7},{7,6},{8,9},{9,8},{10,11... | collective-permute-start | bytes 1572872 | tf_op jit(solution)/shard_map/ppermute | solution.py:392
  394.2 31.8 %collective-permute-start.19 = (bf16[2,512,256]{2,1,0:T(8,128)(2,1)S(1)}, bf16[2,512,256]{2,1,0:T(8,128)(2,1)S(1)}, u32[]{:S(2)}, u32[]{:S(2)}) collective-permute-start(bf16[2,512,256]{2,1,0:T(8,128)(2,1)S(1)} %copy-done.16), channel_id=1, source_target_pairs={{0,1},{1,0},{2,3},{3,2},{4,5},{5,4},{6,7},{7,6},{8,9},{9,8},{10,11... | collective-permute-start | bytes 1572872 | tf_op jit(solution)/shard_map/ppermute | solution.py:392
  407.6 5.5 %collective-permute-start.14 = (bf16[2,128,512]{2,1,0:T(8,128)(2,1)}, bf16[2,128,512]{2,1,0:T(8,128)(2,1)S(1)}, u32[]{:S(2)}, u32[]{:S(2)}) collective-permute-start(bf16[2,128,512]{2,1,0:T(8,128)(2,1)} %get-tuple-element.73), channel_id=1, source_target_pairs={{0,8},{8,16},{16,24},{1,9},{9,17},{17,25},{2,10},{10,18},{18,26},{... | collective-permute-start | bytes 786440 | tf_op jit(solution)/shard_map/ppermute | solution.py:386
  409.5 8.3 %collective-permute-start.15 = (bf16[2,128,512]{2,1,0:T(8,128)(2,1)}, bf16[2,128,512]{2,1,0:T(8,128)(2,1)S(1)}, u32[]{:S(2)}, u32[]{:S(2)}) collective-permute-start(bf16[2,128,512]{2,1,0:T(8,128)(2,1)} %get-tuple-element.74), channel_id=1, source_target_pairs={{8,0},{16,8},{24,16},{9,1},{17,9},{25,17},{10,2},{18,10},{26,18},{... | collective-permute-start | bytes 786440 | tf_op jit(solution)/shard_map/ppermute | solution.py:387
  413.1 4.7 copy-start.24
  423.3 38.1 %collective-permute-start.16 = (bf16[2,512,128]{2,1,0:T(8,128)(2,1)}, bf16[2,512,128]{2,1,0:T(8,128)(2,1)S(1)}, u32[]{:S(2)}, u32[]{:S(2)}) collective-permute-start(bf16[2,512,128]{2,1,0:T(8,128)(2,1)} %get-tuple-element.76), channel_id=1, source_target_pairs={{0,2},{1,3},{2,4},{3,5},{4,6},{5,7},{8,10},{9,11},{10,12},{11,13},... | collective-permute-start | bytes 786440 | tf_op jit(solution)/shard_map/ppermute | solution.py:389
  424.6 38.8 %collective-permute-start.17 = (bf16[2,512,128]{2,1,0:T(8,128)(2,1)}, bf16[2,512,128]{2,1,0:T(8,128)(2,1)S(1)}, u32[]{:S(2)}, u32[]{:S(2)}) collective-permute-start(bf16[2,512,128]{2,1,0:T(8,128)(2,1)} %get-tuple-element.77), channel_id=1, source_target_pairs={{2,0},{3,1},{4,2},{5,3},{6,4},{7,5},{10,8},{11,9},{12,10},{13,11},... | collective-permute-start | bytes 786440 | tf_op jit(solution)/shard_map/ppermute | solution.py:390
  429.1 4.3 collective-permute-start.20
  431.0 6.9 %collective-permute-start.21 = (bf16[1,128,512]{2,1,0:T(8,128)(2,1)}, bf16[1,128,512]{2,1,0:T(8,128)(2,1)S(1)}, u32[]{:S(2)}, u32[]{:S(2)}) collective-permute-start(bf16[1,128,512]{2,1,0:T(8,128)(2,1)} %get-tuple-element.84), channel_id=1, source_target_pairs={{8,0},{16,8},{24,16},{9,1},{17,9},{25,17},{10,2},{18,10},{26,18},{... | collective-permute-start | bytes 393224 | tf_op jit(solution)/shard_map/ppermute | solution.py:387
  433.5 4.5 copy-start.31
  442.2 34.8 %collective-permute-start.22 = (bf16[1,512,128]{2,1,0:T(8,128)(2,1)}, bf16[1,512,128]{2,1,0:T(8,128)(2,1)S(1)}, u32[]{:S(2)}, u32[]{:S(2)}) collective-permute-start(bf16[1,512,128]{2,1,0:T(8,128)(2,1)} %get-tuple-element.86), channel_id=1, source_target_pairs={{0,2},{1,3},{2,4},{3,5},{4,6},{5,7},{8,10},{9,11},{10,12},{11,13},... | collective-permute-start | bytes 393224 | tf_op jit(solution)/shard_map/ppermute | solution.py:389
  446.1 30.8 %collective-permute-start.23 = (bf16[1,512,128]{2,1,0:T(8,128)(2,1)}, bf16[1,512,128]{2,1,0:T(8,128)(2,1)S(1)}, u32[]{:S(2)}, u32[]{:S(2)}) collective-permute-start(bf16[1,512,128]{2,1,0:T(8,128)(2,1)} %get-tuple-element.87), channel_id=1, source_target_pairs={{2,0},{3,1},{4,2},{5,3},{6,4},{7,5},{10,8},{11,9},{12,10},{13,11},... | collective-permute-start | bytes 393224 | tf_op jit(solution)/shard_map/ppermute | solution.py:390
  456.9 13.0 %collective-permute-start.25 = (bf16[1,128,512]{2,1,0:T(8,128)(2,1)}, bf16[1,128,512]{2,1,0:T(8,128)(2,1)S(1)}, u32[]{:S(2)}, u32[]{:S(2)}) collective-permute-start(bf16[1,128,512]{2,1,0:T(8,128)(2,1)} %get-tuple-element.92), channel_id=1, source_target_pairs={{0,8},{8,16},{16,24},{1,9},{9,17},{17,25},{2,10},{10,18},{18,26},{... | collective-permute-start | bytes 393224 | tf_op jit(solution)/shard_map/ppermute | solution.py:386
  461.5 2.0 copy-start.17
  461.5 8.5 %collective-permute-start.26 = (bf16[1,128,512]{2,1,0:T(8,128)(2,1)}, bf16[1,128,512]{2,1,0:T(8,128)(2,1)S(1)}, u32[]{:S(2)}, u32[]{:S(2)}) collective-permute-start(bf16[1,128,512]{2,1,0:T(8,128)(2,1)} %get-tuple-element.93), channel_id=1, source_target_pairs={{8,0},{16,8},{24,16},{9,1},{17,9},{25,17},{10,2},{18,10},{26,18},{... | collective-permute-start | bytes 393224 | tf_op jit(solution)/shard_map/ppermute | solution.py:387
  468.7 26.7 %collective-permute-start.29 = (bf16[2,512,256]{2,1,0:T(8,128)(2,1)}, bf16[2,512,256]{2,1,0:T(8,128)(2,1)S(1)}, u32[]{:S(2)}, u32[]{:S(2)}) collective-permute-start(bf16[2,512,256]{2,1,0:T(8,128)(2,1)} %get-tuple-element.98), channel_id=1, source_target_pairs={{0,1},{1,0},{2,3},{3,2},{4,5},{5,4},{6,7},{7,6},{8,9},{9,8},{10,11... | collective-permute-start | bytes 1572872 | tf_op jit(solution)/shard_map/ppermute | solution.py:392
  474.2 7.3 %collective-permute-start.27 = (bf16[1,512,128]{2,1,0:T(8,128)(2,1)}, bf16[1,512,128]{2,1,0:T(8,128)(2,1)S(1)}, u32[]{:S(2)}, u32[]{:S(2)}) collective-permute-start(bf16[1,512,128]{2,1,0:T(8,128)(2,1)} %get-tuple-element.95), channel_id=1, source_target_pairs={{0,2},{1,3},{2,4},{3,5},{4,6},{5,7},{8,10},{9,11},{10,12},{11,13},... | collective-permute-start | bytes 393224 | tf_op jit(solution)/shard_map/ppermute | solution.py:389
  475.4 7.5 %collective-permute-start.28 = (bf16[1,512,128]{2,1,0:T(8,128)(2,1)}, bf16[1,512,128]{2,1,0:T(8,128)(2,1)S(1)}, u32[]{:S(2)}, u32[]{:S(2)}) collective-permute-start(bf16[1,512,128]{2,1,0:T(8,128)(2,1)} %get-tuple-element.96), channel_id=1, source_target_pairs={{2,0},{3,1},{4,2},{5,3},{6,4},{7,5},{10,8},{11,9},{12,10},{13,11},... | collective-permute-start | bytes 393224 | tf_op jit(solution)/shard_map/ppermute | solution.py:390
  481.2 6.4 %collective-permute-start.30 = (bf16[1,512,256]{2,1,0:T(8,128)(2,1)}, bf16[1,512,256]{2,1,0:T(8,128)(2,1)S(1)}, u32[]{:S(2)}, u32[]{:S(2)}) collective-permute-start(bf16[1,512,256]{2,1,0:T(8,128)(2,1)} %get-tuple-element.99), channel_id=1, source_target_pairs={{0,1},{1,0},{2,3},{3,2},{4,5},{5,4},{6,7},{7,6},{8,9},{9,8},{10,11... | collective-permute-start | bytes 786440 | tf_op jit(solution)/shard_map/ppermute | solution.py:392
  487.2 8.3 %collective-permute-start.31 = (bf16[1,512,256]{2,1,0:T(8,128)(2,1)}, bf16[1,512,256]{2,1,0:T(8,128)(2,1)S(1)}, u32[]{:S(2)}, u32[]{:S(2)}) collective-permute-start(bf16[1,512,256]{2,1,0:T(8,128)(2,1)} %get-tuple-element.100), channel_id=1, source_target_pairs={{0,1},{1,0},{2,3},{3,2},{4,5},{5,4},{6,7},{7,6},{8,9},{9,8},{10,11... | collective-permute-start | bytes 786440 | tf_op jit(solution)/shard_map/ppermute | solution.py:392
  487.6 7.8 %copy-start.8 = (bf16[1,512,256]{2,1,0:T(8,128)(2,1)}, bf16[1,512,256]{2,1,0:T(8,128)(2,1)S(1)}, u32[]{:S(2)}) copy-start(bf16[1,512,256]{2,1,0:T(8,128)(2,1)S(1)} %collective-permute-done.30.refs_8_) | copy-start | bytes 786436
  (24 other events, 22.1 us)
Sparse Core Ops, SparseCore 0:
  18.7 146.3 reduce-scatter.5
  167.4 77.6 reduce-scatter.7
  270.3 84.9 reduce-scatter.9
  357.4 46.0 reduce-scatter.11
  405.7 48.7 reduce-scatter.13

commit v2 on v1

--- a/solution.py
+++ b/solution.py
@@ -169,11 +169,12 @@
     return (gaussian + diagonal).astype(jnp.bfloat16)
 
 
-def smooth_x(scaled, before, after, tiles_x, labels, first):
+def smooth_x(scaled, before, after, tiles_x, labels, first, behind=()):
     slots, slab_x, wide = scaled.shape
     classes, tiles, rows, window = tiles_x.shape
 
-    def body(mid_ref, before_ref, after_ref, tiles_ref, label_ref, out_ref, low_ref, high_ref, cat_ref):
+    def body(mid_ref, before_ref, after_ref, tiles_ref, label_ref, *refs):
+        out_ref, low_ref, high_ref, cat_ref = refs[len(behind) :]
         cat_ref[:BAND] = before_ref[0]
         cat_ref[BAND : BAND + slab_x] = mid_ref[0]
         cat_ref[BAND + slab_x :] = after_ref[0]
@@ -202,7 +203,8 @@
             edge,
             pl.BlockSpec(tiles_x.shape, lambda m: (0, 0, 0, 0)),
             pl.BlockSpec((1, 1, wide), lambda m: (first + m, 0, 0)),
-        ],
+        ]
+        + [pl.BlockSpec(memory_space=pl.ANY)] * len(behind),
         out_specs=[full, side, side],
         out_shape=[
             jax.ShapeDtypeStruct((slots, slab_x, wide), jnp.bfloat16),
@@ -213,14 +215,15 @@
         compiler_params=params(),
         cost_estimate=cost(2 * classes * window * size, 6 * size, size),
         name="smooth_x",
-    )(scaled, before, after, tiles_x, labels)
-
-
-def smooth_y(bounded, before, after, tiles_y, labels, place, first):
+    )(scaled, before, after, tiles_x, labels, *behind)
+
+
+def smooth_y(bounded, before, after, tiles_y, labels, place, first, behind=()):
     slots, slab_x, wide = bounded.shape
     classes, tiles, window, narrow = tiles_y.shape
 
-    def body(place_ref, mid_ref, before_ref, after_ref, tiles_ref, label_ref, keep_ref, send_ref, cat_ref):
+    def body(place_ref, mid_ref, before_ref, after_ref, tiles_ref, label_ref, *refs):
+        keep_ref, send_ref, cat_ref = refs[len(behind) :]
         cat_ref[:, :BAND] = before_ref[0]
         cat_ref[:, BAND : BAND + wide] = mid_ref[0]
         cat_ref[:, BAND + wide :] = after_ref[0]
@@ -253,7 +256,8 @@
                 side,
                 pl.BlockSpec(tiles_y.shape, lambda m, place_ref: (0, 0, 0, 0)),
                 pl.BlockSpec((1, slab_x, 1), lambda m, place_ref: (first + m, 0, 0)),
-            ],
+            ]
+            + [pl.BlockSpec(memory_space=pl.ANY)] * len(behind),
             out_specs=[block, block],
             scratch_shapes=[pltpu.VMEM((slab_x, wide + 2 * BAND), jnp.bfloat16)],
         ),
@@ -261,7 +265,7 @@
         compiler_params=params(),
         cost_estimate=cost(2 * classes * window * size, 6 * size),
         name="smooth_y",
-    )(place, bounded, before, after, tiles_y, labels)
+    )(place, bounded, before, after, tiles_y, labels, *behind)
 
 
 def join_planes(kept, came, perm_back, slots_of, planes, rows):
@@ -337,8 +341,8 @@
     lit_planes = jnp.transpose(illumination, (1, 0, 2))
     lit = lax.dynamic_slice_in_dim(lit_planes, half * pair, half, 0)
     lit_sent = lax.dynamic_slice_in_dim(lit_planes, half * (1 - pair), half, 0).astype(jnp.bfloat16)
+
     lit_pair = lax.ppermute(lit_sent, "ev", other)
-
     split, before = {}, []
     for some in (chunks[:1], chunks[1:2], chunks[2:]):
         for k in range(kernels):
@@ -363,46 +367,65 @@
     tiles_x = band_tiles(full_x, widths_x, lax.axis_index("gx") * slab_x, slab_x // tile, tile)
     tiles_y = jnp.swapaxes(band_tiles(full_y, widths_y, line * PAIR * slab_y, PAIR, slab_y), 2, 3)
 
-    own, sent = split[chunks[1]]
-    split[chunks[1]] = own, hold(sent, [lit_pair, split[chunks[2]][0]])
-
-    slots_of, sums, kept, came = {}, {}, {}, {}
+    slots_of, added, sums, kept, came = {}, {}, {}, {}, {}
     for n, (order, k, first, slots) in enumerate(chunks):
         for m in range(slots):
             slots_of[k * half + first + m] = (n, m)
 
-    def begin(n, after=()):
+    def begin(n, after=(), behind=()):
         order, k, first, slots = chunks[n]
         if order == "yz":
             own, sent = split[chunks[n]]
-            sums[n] = [over_line(add_parts(own, lax.ppermute(sent, "ev", other), after))]
+            if behind:
+                sent = hold(sent, behind)
+            added[n] = add_parts(own, lax.ppermute(sent, "ev", other), after)
+            sums[n] = [over_line(added[n])]
         else:
             both = over_line(split[chunks[n]][0])
             sums[n] = [both[:slots], lax.ppermute(both[slots:], "ev", other)]
 
-    def finish(n, after=()):
+    scaled, sides = {}, {}
+
+    def divide(n, after=()):
         order, k, first, slots = chunks[n]
-        scaled, top, bottom = scale(sums[n], lit, lit_pair, place, first, after)
-        before = lax.ppermute(bottom, "gx", x_up)
-        after = lax.ppermute(top, "gx", x_down)
-        bounded, low, high = smooth_x(scaled, before, after, tiles_x, labels_x, first)
-        before = lax.ppermute(high, "ev", z_up)
-        after = lax.ppermute(low, "ev", z_down)
-        kept[n], send = smooth_y(bounded, before, after, tiles_y, labels_y, place, first)
+        scaled[n], top, bottom = scale(sums[n], lit, lit_pair, place, first, after)
+        sides[n] = lax.ppermute(bottom, "gx", x_up), lax.ppermute(top, "gx", x_down)
+
+    bounded, ends = {}, {}
+
+    def cross_x(n, after=()):
+        order, k, first, slots = chunks[n]
+        bounded[n], low, high = smooth_x(scaled[n], *sides[n], tiles_x, labels_x, first, after)
+        ends[n] = lax.ppermute(high, "ev", z_up), lax.ppermute(low, "ev", z_down)
+
+    def cross_y(n, after=()):
+        order, k, first, slots = chunks[n]
+        kept[n], send = smooth_y(bounded[n], *ends[n], tiles_y, labels_y, place, first, after)
         came[n] = lax.ppermute(send, "ev", other)
 
     last = len(chunks)
     begin(0)
-    begin(1)
-    begin(2, [sums[0][1]])
-    finish(1)
-    begin(3, [kept[1]])
-    finish(0)
+    begin(1, [split[c][0] for c in chunks[2:]], [lit_pair, labels_pair])
+    begin(2, [sums[0][0]])
+    divide(1)
+    cross_x(1)
+    cross_y(1)
+    begin(3, [kept[1], sums[0][1]])
+    divide(0)
+    cross_x(0)
+    cross_y(0)
     for n in range(4, last):
         begin(n, [kept[0]])
-    finish(2, [kept[0], came[1]])
-    for n in range(3, last):
-        finish(n, [came[0]])
+    divide(2)
+    divide(3, [came[1]])
+    cross_x(2, [scaled[3]])
+    cross_x(3)
+    cross_y(2, [bounded[3]])
+    cross_y(3)
+    for n in range(4, last):
+        divide(n, [kept[n - 1], came[0], came[2]])
+        cross_x(n)
+        cross_y(n)
     order = range(last)
     return join_planes([kept[n] for n in order], [came[n] for n in order], perm.T, slots_of, planes, slab_x // 2)
 

time: 509 us -> 490 us (0.963)
  waiting for transfers between devices: 281 us -> 260 us
    ppermute x1, waiting for transfers between devices: 22.4 us -> 6.29 us  [begin(): sums[n] = [both[:slots], lax.ppermute(both[slots:], 'ev', other)]]
    ppermute x1, waiting for transfers between devices: 0.01 us -> 11.9 us  [per_device(): labels_pair = lax.ppermute(labels_sent, 'ev', other)]
    ppermute x29, waiting for transfers between devices: 234 us -> 224 us  [the longest x4 146 us: begin(): added[n] = add_parts(own, lax.ppermute(sent, 'ev', other), after)]
    reduce_scatter x5, waiting for transfers between devices: 23.9 us -> 17.5 us  [over_line(): lax.psum_scatter(parts, 'ev', scatter_dimension=0, axis_index_groups=line...]
    unnamed x72 -> x84, local copies, waits for them, and re-layouts: 16.8 us -> 14.2 us
  transfers between devices with their start and end apart: 37 -> 37, of which waited for: 19 -> 21; matrix products, arithmetic and copies ran while one was open for 4% -> 4% of each run, Pallas kernels for 21% -> 20%
where the time goes in v2:
time: 490 us; the launch traced here: 488 us
  waiting for transfers between devices  260 us (53%)
  Pallas kernels  120 us (24%)
  starting transfers between devices  61.7 us (13%)
  local copies, waits for them, and re-layouts  23.9 us (5%)
  between operations  13.6 us (3%)
  other arithmetic  8.73 us (2%)
    ppermute x4, waiting for transfers between devices, begin(): added[n] = add_parts(own, lax.ppermute(sent, 'ev', other), after)  146 us
    ppermute x10, waiting for transfers between devices, cross_x(): ends[n] = (lax.ppermute(high, 'ev', z_up), lax.ppermute(low, 'ev', z_down))  50.9 us
    pallas_call x3, Pallas kernels, split_planes(): pl.pallas_call(body, grid=(shards, slab_x // rows), in_specs=[pl.BlockSpe...  35.4 us
    pallas_call x4, Pallas kernels, add_parts(): pl.pallas_call(body, grid=(shards, slots), in_specs=[spec, spec] + [pl.Bl...  24.4 us
    ppermute x5, starting transfers between devices, divide(): lax.ppermute(bottom, 'gx', x_up)  23 us
    pallas_call x5, Pallas kernels, smooth_x(): pl.pallas_call(body, grid=(slots,), in_specs=[full, edge, edge, pl.BlockS...  21.7 us
    pallas_call x5, Pallas kernels, smooth_y(): pl.pallas_call(body, grid_spec=pltpu.PrefetchScalarGridSpec(num_scalar_pr...  21 us
    ppermute x10, starting transfers between devices, cross_x(): ends[n] = (lax.ppermute(high, 'ev', z_up), lax.ppermute(low, 'ev', z_down))  18.6 us
  transfers between devices with their start and end apart: 37, of which 21 were waited for; matrix products, arithmetic and copies ran while one was open for 4% of the time, Pallas kernels for 20%

profile of v2, /device:TPU:1, one launch (start us, length us, event | category | flops | bytes accessed | tf_op | source)
XLA Modules:
  0.0 488.5 jit_solution(5966736955103073694)
XLA Ops:
  7.5 11.1 %split_planes.3.refs_0_ = bf16[4,4,512,512]{3,2,1,0:T(8,128)(2,1)} custom-call(bf16[1,512,2,8,2048]{4,3,2,1,0:T(8,128)(2,1)} %part_ref.5, bf16[256,256]{1,0:T(8,128)(2,1)} %get-tuple-element.106.perm_ref), custom_call_target="tpu_custom_call" | custom-call | tf_op jit(solution)/shard_map/split_planes/pallas_call | solution.py:63
  18.6 2.6 constant_dynamic-slice_fusion.2
  23.6 11.1 %split_planes.4 = (bf16[4,2,512,512]{3,2,1,0:T(8,128)(2,1)}, bf16[4,2,512,512]{3,2,1,0:T(8,128)(2,1)}) custom-call(bf16[1,512,2,8,2048]{4,3,2,1,0:T(8,128)(2,1)} %part_ref.5, bf16[256,256]{1,0:T(8,128)(2,1)} %get-tuple-element.106.perm_ref, bf16[4,4,512,512]{3,2,1,0:T(8,128)(2,1)} %split_planes.3.refs_0_), custom_call_target="tpu_custom_call" | custom-call | tf_op jit(solution)/shard_map/split_planes/pallas_call | solution.py:63
  34.7 11.9 %collective-permute-done.4.refs_2_ = s32[4,256]{1,0:T(4,128)S(1)} collective-permute-done((s32[4,256]{1,0:T(4,128)S(1)}, s32[4,256]{1,0:T(4,128)S(1)}, u32[]{:S(2)}, u32[]{:S(2)}) %collective-permute-start.4) | collective-permute-done | bytes 4128 | tf_op jit(solution)/shard_map/ppermute | solution.py:358
  48.8 13.2 %split_planes.5 = (bf16[4,2,512,512]{3,2,1,0:T(8,128)(2,1)}, bf16[4,2,512,512]{3,2,1,0:T(8,128)(2,1)}, bf16[4,1,512,512]{3,2,1,0:T(8,128)(2,1)}, bf16[4,1,512,51...) custom-call(bf16[1,512,2,8,2048]{4,3,2,1,0:T(8,128)(2,1)} %part_ref.5, ...), custom_call_target="tpu_custom_call" | custom-call | tf_op jit(solution)/shard_map/split_planes/pallas_call | solution.py:63
  62.0 76.9 %collective-permute-done.7.b_ref = bf16[4,2,512,512]{3,2,1,0:T(8,128)(2,1)} collective-permute-done((bf16[4,2,512,512]{3,2,1,0:T(8,128)(2,1)}, bf16[4,2,512,512]{3,2,1,0:T(8,128)(2,1)}, u32[]{:S(2)}, u32[]{:S(2)}) %collective-permute-start.7) | collective-permute-done | bytes 4194336 | tf_op jit(solution)/shard_map/ppermute | solution.py:381
  138.9 7.8 %add_parts.4 = bf16[4,2,512,512]{3,2,1,0:T(8,128)(2,1)} custom-call(bf16[4,2,512,512]{3,2,1,0:T(8,128)(2,1)} %get-tuple-element.60.refs_0_.a_ref, bf16[4,2,512,512]{3,2,1,0:T(8,128)(2,1)} %collective-permute-done.7.b_ref, bf16[4,2,512,512]{3,2,1,0:T(8,128)(2,1)} %get-tuple-element.62.refs_0_.a_ref, bf16[4,1,512,512]{3,2,1,0:T(8,128)(2,1)} %get-tuple-element.63.refs_1_.a_ref, ...), custom_call_target="tpu_custom_call" | custom-call | flops 2097152 | bytes 12582912 | tf_op jit(solution)/shard_map/add_parts/pallas_call | solution.py:104
  147.6 17.5 %reduce-scatter.6.cloned.1.call-done = bf16[1,4,512,512]{3,2,1,0:T(8,128)(2,1)} async-done(((bf16[4,4,512,512]{3,2,1,0:T(8,128)(2,1)}), bf16[1,4,512,512]{3,2,1,0:T(8,128)(2,1)}) %reduce-scatter.6.cloned.1.call-update) | async-done | bytes 2097168 | tf_op jit(solution)/shard_map/reduce_scatter | solution.py:329
  165.1 3.1 slice_bitcast_fusion
  168.2 69.1 %collective-permute-done.12.b_ref = bf16[4,2,512,512]{3,2,1,0:T(8,128)(2,1)} collective-permute-done((bf16[4,2,512,512]{3,2,1,0:T(8,128)(2,1)}, bf16[4,2,512,512]{3,2,1,0:T(8,128)(2,1)}, u32[]{:S(2)}, u32[]{:S(2)}) %collective-permute-start.12) | collective-permute-done | bytes 4194336 | tf_op jit(solution)/shard_map/ppermute | solution.py:381
  237.2 7.9 %add_parts.5 = bf16[4,2,512,512]{3,2,1,0:T(8,128)(2,1)} custom-call(bf16[4,2,512,512]{3,2,1,0:T(8,128)(2,1)} %get-tuple-element.62.refs_0_.a_ref, bf16[4,2,512,512]{3,2,1,0:T(8,128)(2,1)} %collective-permute-done.12.b_ref, bf16[2,512,512]{2,1,0:T(8,128)(2,1)} %get-tuple-element.102.refs_0_), custom_call_target="tpu_custom_call" | custom-call | flops 2097152 | bytes 12582912 | tf_op jit(solution)/shard_map/add_parts/pallas_call | solution.py:104
  249.8 3.1 add_convert_fusion.tiles_ref
  252.9 2.8 scale.6
  255.6 6.7 %collective-permute-start.8 = (bf16[2,128,512]{2,1,0:T(8,128)(2,1)}, bf16[2,128,512]{2,1,0:T(8,128)(2,1)S(1)}, u32[]{:S(2)}, u32[]{:S(2)}) collective-permute-start(bf16[2,128,512]{2,1,0:T(8,128)(2,1)} %get-tuple-element.66), channel_id=1, source_target_pairs={{0,8},{8,16},{16,24},{1,9},{9,17},{17,25},{2,10},{10,18},{18,26},{... | collective-permute-start | bytes 786440 | tf_op jit(solution)/shard_map/ppermute | solution.py:392
  266.5 4.1 collective-permute-done.9.after_ref
  271.4 5.0 %smooth_x.6 = (bf16[2,512,512]{2,1,0:T(8,128)(2,1)}, bf16[2,512,128]{2,1,0:T(8,128)(2,1)}, bf16[2,512,128]{2,1,0:T(8,128)(2,1)}) custom-call(bf16[2,512,512]{2,1,0:T(8,128)(2,1)} %get-tuple-element.65.mid_ref, bf16[2,128,512]{2,1,0:T(8,128)(2,1)} %copy-done.22, bf16[2,128,512]{2,1,0:T(8,128)(2,1)} %copy-done.25, ...), custom_call_target="tpu_custom_call" | custom-call | flops 1610612736 | bytes 3145728 | tf_op jit(solution)/shard_map/smooth_x/pallas_call | solution.py:197
  276.4 3.2 collective-permute-start.10
  285.4 4.9 %collective-permute-done.10.before_ref = bf16[2,512,128]{2,1,0:T(8,128)(2,1)S(1)} collective-permute-done((bf16[2,512,128]{2,1,0:T(8,128)(2,1)}, bf16[2,512,128]{2,1,0:T(8,128)(2,1)S(1)}, u32[]{:S(2)}, u32[]{:S(2)}) %collective-permute-start.10) | collective-permute-done | bytes 262176 | tf_op jit(solution)/shard_map/ppermute | solution.py:399
  290.4 10.9 %collective-permute-done.11.after_ref = bf16[2,512,128]{2,1,0:T(8,128)(2,1)} collective-permute-done((bf16[2,512,128]{2,1,0:T(8,128)(2,1)}, bf16[2,512,128]{2,1,0:T(8,128)(2,1)}, u32[]{:S(2)}, u32[]{:S(2)}) %collective-permute-start.11) | collective-permute-done | bytes 262176 | tf_op jit(solution)/shard_map/ppermute | solution.py:399
  301.3 4.7 smooth_y.6
  306.0 6.3 %collective-permute-done.refs_1_ = bf16[2,512,512]{2,1,0:T(8,128)(2,1)S(1)} collective-permute-done((bf16[2,512,512]{2,1,0:T(8,128)(2,1)}, bf16[2,512,512]{2,1,0:T(8,128)(2,1)S(1)}, u32[]{:S(2)}, u32[]{:S(2)}) %collective-permute-start) | collective-permute-done | bytes 1048608 | tf_op jit(solution)/shard_map/ppermute | solution.py:385
  313.3 4.4 add_parts.6
  317.8 3.2 scale.5
  321.0 7.0 %collective-permute-start.2 = (bf16[2,128,512]{2,1,0:T(8,128)(2,1)}, bf16[2,128,512]{2,1,0:T(8,128)(2,1)S(1)}, u32[]{:S(2)}, u32[]{:S(2)}) collective-permute-start(bf16[2,128,512]{2,1,0:T(8,128)(2,1)} %get-tuple-element.54), channel_id=1, source_target_pairs={{0,8},{8,16},{16,24},{1,9},{9,17},{17,25},{2,10},{10,18},{18,26},{... | collective-permute-start | bytes 786440 | tf_op jit(solution)/shard_map/ppermute | solution.py:392
  331.7 4.6 collective-permute-done.3.after_ref
  337.0 4.8 smooth_x.5
  341.8 3.3 collective-permute-start.5
  346.4 9.3 %collective-permute-done.5.before_ref = bf16[2,512,128]{2,1,0:T(8,128)(2,1)S(1)} collective-permute-done((bf16[2,512,128]{2,1,0:T(8,128)(2,1)}, bf16[2,512,128]{2,1,0:T(8,128)(2,1)S(1)}, u32[]{:S(2)}, u32[]{:S(2)}) %collective-permute-start.5) | collective-permute-done | bytes 262176 | tf_op jit(solution)/shard_map/ppermute | solution.py:399
  355.8 10.1 %collective-permute-done.6.after_ref = bf16[2,512,128]{2,1,0:T(8,128)(2,1)S(1)} collective-permute-done((bf16[2,512,128]{2,1,0:T(8,128)(2,1)}, bf16[2,512,128]{2,1,0:T(8,128)(2,1)S(1)}, u32[]{:S(2)}, u32[]{:S(2)}) %collective-permute-start.6) | collective-permute-done | bytes 262176 | tf_op jit(solution)/shard_map/ppermute | solution.py:399
  366.6 4.6 smooth_y.5
  372.6 4.4 add_parts.7
  377.5 2.7 scale.7
  384.6 3.4 collective-permute-done.16.refs_3_.refs_6_
  392.0 4.9 smooth_x.7
  396.8 2.9 collective-permute-start.17
  406.5 3.6 collective-permute-done.20.after_ref
  410.8 3.5 smooth_x.8
  414.3 7.5 %collective-permute-done.18.after_ref = bf16[2,512,128]{2,1,0:T(8,128)(2,1)S(1)} collective-permute-done((bf16[2,512,128]{2,1,0:T(8,128)(2,1)}, bf16[2,512,128]{2,1,0:T(8,128)(2,1)S(1)}, u32[]{:S(2)}, u32[]{:S(2)}) %collective-permute-start.18) | collective-permute-done | bytes 262176 | tf_op jit(solution)/shard_map/ppermute | solution.py:399
  422.6 4.7 smooth_y.7
  432.8 2.9 collective-permute-done.22.after_ref
  436.4 3.5 smooth_y.8
  443.3 4.5 collective-permute-start.26
  450.1 4.3 collective-permute-done.27.after_ref
  455.0 3.5 smooth_x.9
  462.6 3.2 collective-permute-done.29.after_ref
  466.4 3.5 smooth_y.9
  471.2 5.7 %collective-permute-done.31.refs_9_ = bf16[1,512,256]{2,1,0:T(8,128)(2,1)S(1)} collective-permute-done((bf16[1,512,256]{2,1,0:T(8,128)(2,1)}, bf16[1,512,256]{2,1,0:T(8,128)(2,1)S(1)}, u32[]{:S(2)}, u32[]{:S(2)}) %collective-permute-start.31) | collective-permute-done | bytes 262176 | tf_op jit(solution)/shard_map/ppermute | solution.py:404
  477.6 4.4 join_planes.1
  (159 shorter events, 66.7 us)
Async XLA Ops:
  6.5 277.4 %copy-start = (s32[512,8]{0,1:T(8,128)S(1)}, s32[512,8]{0,1:T(8,128)}, u32[]{:S(2)}) copy-start(s32[512,8]{0,1:T(8,128)} %param.9) | copy-start | bytes 49156
  6.5 158.6 %reduce-scatter.6.cloned.1.call-start = ((), (), s32[]{:S(2)}) async-start(), calls=%async_computation.5 | async-start | bytes 10485760 | tf_op jit(solution)/shard_map/reduce_scatter | solution.py:329
  18.6 234.3 %reduce-scatter.8.cloned.1.call-start = ((), (), s32[]{:S(2)}) async-start(), calls=%async_computation.6 | async-start | bytes 5242880 | tf_op jit(solution)/shard_map/reduce_scatter | solution.py:329
  21.4 25.2 %collective-permute-start.1 = (bf16[4,512,256]{2,1,0:T(8,128)(2,1)S(1)}, bf16[4,512,256]{2,1,0:T(8,128)(2,1)S(1)}, u32[]{:S(2)}, u32[]{:S(2)}) collective-permute-start(bf16[4,512,256]{2,1,0:T(8,128)(2,1)S(1)} %bitcast.26), channel_id=1, source_target_pairs={{0,1},{1,0},{2,3},{3,2},{4,5},{5,4},{6,7},{7,6},{8,9},{9,8},{10,11... | collective-permute-start | bytes 3145736 | tf_op jit(solution)/shard_map/ppermute | solution.py:345
  23.5 23.1 %collective-permute-start.4 = (s32[4,256]{1,0:T(4,128)S(1)}, s32[4,256]{1,0:T(4,128)S(1)}, u32[]{:S(2)}, u32[]{:S(2)}) collective-permute-start(s32[4,256]{1,0:T(4,128)S(1)} %get-tuple-element.104), channel_id=1, source_target_pairs={{0,1},{1,0},{2,3},{3,2},{4,5},{5,4},{6,7},{7,6},{8,9},{9,8},{10,11... | collective-permute-start | bytes 12296 | tf_op jit(solution)/shard_map/ppermute | solution.py:358
  47.6 91.3 %collective-permute-start.7 = (bf16[4,2,512,512]{3,2,1,0:T(8,128)(2,1)}, bf16[4,2,512,512]{3,2,1,0:T(8,128)(2,1)}, u32[]{:S(2)}, u32[]{:S(2)}) collective-permute-start(bf16[4,2,512,512]{3,2,1,0:T(8,128)(2,1)} %hold.1), channel_id=1, source_target_pairs={{0,1},{1,0},{2,3},{3,2},{4,5},{5,4},{6,7},{7,6},{8,9},{9,8},{10,11... | collective-permute-start | bytes 12582920 | tf_op jit(solution)/shard_map/ppermute | solution.py:381
  146.8 230.8 %reduce-scatter.10.cloned.1.call-start = ((), (), s32[]{:S(2)}) async-start(), calls=%async_computation.7 | async-start | bytes 5242880 | tf_op jit(solution)/shard_map/reduce_scatter | solution.py:329
  146.8 90.4 %collective-permute-start.12 = (bf16[4,2,512,512]{3,2,1,0:T(8,128)(2,1)}, bf16[4,2,512,512]{3,2,1,0:T(8,128)(2,1)}, u32[]{:S(2)}, u32[]{:S(2)}) collective-permute-start(bf16[4,2,512,512]{3,2,1,0:T(8,128)(2,1)} %get-tuple-element.72), channel_id=1, source_target_pairs={{0,1},{1,0},{2,3},{3,2},{4,5},{5,4},{6,7},{7,6},{8,9},{9,8},{10,11... | collective-permute-start | bytes 12582920 | tf_op jit(solution)/shard_map/ppermute | solution.py:381
  245.1 142.8 %reduce-scatter.12.cloned.1.call-start = ((), (), s32[]{:S(2)}) async-start(), calls=%async_computation.8 | async-start | bytes 2621440 | tf_op jit(solution)/shard_map/reduce_scatter | solution.py:329
  245.2 60.8 %collective-permute-start.15 = (bf16[4,1,512,512]{3,2,1,0:T(8,128)(2,1)}, bf16[4,1,512,512]{3,2,1,0:T(8,128)(2,1)S(1)}, u32[]{:S(2)}, u32[]{:S(2)}) collective-permute-start(bf16[4,1,512,512]{3,2,1,0:T(8,128)(2,1)} %get-tuple-element.76), channel_id=1, source_target_pairs={{0,1},{1,0},{2,3},{3,2},{4,5},{5,4},{6,7},{7,6},{8,9},{9,8},{10,11... | collective-permute-start | bytes 6291464 | tf_op jit(solution)/shard_map/ppermute | solution.py:381
  252.9 13.1 %copy-start.15 = (s32[4,256]{1,0:T(4,128)S(1)}, s32[4,256]{1,0:T(4,128)}, u32[]{:S(2)}) copy-start(s32[4,256]{1,0:T(4,128)} %copy-done.14) | copy-start | bytes 12292
  255.6 10.9 %collective-permute-start.8 = (bf16[2,128,512]{2,1,0:T(8,128)(2,1)}, bf16[2,128,512]{2,1,0:T(8,128)(2,1)S(1)}, u32[]{:S(2)}, u32[]{:S(2)}) collective-permute-start(bf16[2,128,512]{2,1,0:T(8,128)(2,1)} %get-tuple-element.66), channel_id=1, source_target_pairs={{0,8},{8,16},{16,24},{1,9},{9,17},{17,25},{2,10},{10,18},{18,26},{... | collective-permute-start | bytes 786440 | tf_op jit(solution)/shard_map/ppermute | solution.py:392
  262.4 8.3 %collective-permute-start.9 = (bf16[2,128,512]{2,1,0:T(8,128)(2,1)}, bf16[2,128,512]{2,1,0:T(8,128)(2,1)S(1)}, u32[]{:S(2)}, u32[]{:S(2)}) collective-permute-start(bf16[2,128,512]{2,1,0:T(8,128)(2,1)} %get-tuple-element.67), channel_id=1, source_target_pairs={{8,0},{16,8},{24,16},{9,1},{17,9},{25,17},{10,2},{18,10},{26,18},{... | collective-permute-start | bytes 786440 | tf_op jit(solution)/shard_map/ppermute | solution.py:392
  276.4 14.0 %collective-permute-start.10 = (bf16[2,512,128]{2,1,0:T(8,128)(2,1)}, bf16[2,512,128]{2,1,0:T(8,128)(2,1)S(1)}, u32[]{:S(2)}, u32[]{:S(2)}) collective-permute-start(bf16[2,512,128]{2,1,0:T(8,128)(2,1)} %get-tuple-element.69), channel_id=1, source_target_pairs={{0,2},{1,3},{2,4},{3,5},{4,6},{5,7},{8,10},{9,11},{10,12},{11,13},... | collective-permute-start | bytes 786440 | tf_op jit(solution)/shard_map/ppermute | solution.py:399
  279.6 21.7 %collective-permute-start.11 = (bf16[2,512,128]{2,1,0:T(8,128)(2,1)}, bf16[2,512,128]{2,1,0:T(8,128)(2,1)}, u32[]{:S(2)}, u32[]{:S(2)}) collective-permute-start(bf16[2,512,128]{2,1,0:T(8,128)(2,1)} %get-tuple-element.70), channel_id=1, source_target_pairs={{2,0},{3,1},{4,2},{5,3},{6,4},{7,5},{10,8},{11,9},{12,10},{13,11},... | collective-permute-start | bytes 786440 | tf_op jit(solution)/shard_map/ppermute | solution.py:399
  281.1 31.2 %collective-permute-start = (bf16[2,512,512]{2,1,0:T(8,128)(2,1)}, bf16[2,512,512]{2,1,0:T(8,128)(2,1)S(1)}, u32[]{:S(2)}, u32[]{:S(2)}) collective-permute-start(bf16[2,512,512]{2,1,0:T(8,128)(2,1)} %get-tuple-element.101), channel_id=1, source_target_pairs={{0,1},{1,0},{2,3},{3,2},{4,5},{5,4},{6,7},{7,6},{8,9},{9,8},{10,11... | collective-permute-start | bytes 3145736 | tf_op jit(solution)/shard_map/ppermute | solution.py:385
  290.4 10.9 %copy-start.23 = (bf16[2,512,128]{2,1,0:T(8,128)(2,1)}, bf16[2,512,128]{2,1,0:T(8,128)(2,1)S(1)}, u32[]{:S(2)}) copy-start(bf16[2,512,128]{2,1,0:T(8,128)(2,1)S(1)} %collective-permute-done.10.before_ref) | copy-start | bytes 786436
  317.7 122.2 %reduce-scatter.14.cloned.1.call-start = ((), (), s32[]{:S(2)}) async-start(), calls=%async_computation.9 | async-start | bytes 2621440 | tf_op jit(solution)/shard_map/reduce_scatter | solution.py:329
  317.7 53.5 %collective-permute-start.23 = (bf16[4,1,512,512]{3,2,1,0:T(8,128)(2,1)}, bf16[4,1,512,512]{3,2,1,0:T(8,128)(2,1)S(1)}, u32[]{:S(2)}, u32[]{:S(2)}) collective-permute-start(bf16[4,1,512,512]{3,2,1,0:T(8,128)(2,1)} %get-tuple-element.89), channel_id=1, source_target_pairs={{0,1},{1,0},{2,3},{3,2},{4,5},{5,4},{6,7},{7,6},{8,9},{9,8},{10,11... | collective-permute-start | bytes 6291464 | tf_op jit(solution)/shard_map/ppermute | solution.py:381
  321.0 10.7 %collective-permute-start.2 = (bf16[2,128,512]{2,1,0:T(8,128)(2,1)}, bf16[2,128,512]{2,1,0:T(8,128)(2,1)S(1)}, u32[]{:S(2)}, u32[]{:S(2)}) collective-permute-start(bf16[2,128,512]{2,1,0:T(8,128)(2,1)} %get-tuple-element.54), channel_id=1, source_target_pairs={{0,8},{8,16},{16,24},{1,9},{9,17},{17,25},{2,10},{10,18},{18,26},{... | collective-permute-start | bytes 786440 | tf_op jit(solution)/shard_map/ppermute | solution.py:392
  328.1 8.2 %collective-permute-start.3 = (bf16[2,128,512]{2,1,0:T(8,128)(2,1)}, bf16[2,128,512]{2,1,0:T(8,128)(2,1)S(1)}, u32[]{:S(2)}, u32[]{:S(2)}) collective-permute-start(bf16[2,128,512]{2,1,0:T(8,128)(2,1)} %get-tuple-element.55), channel_id=1, source_target_pairs={{8,0},{16,8},{24,16},{9,1},{17,9},{25,17},{10,2},{18,10},{26,18},{... | collective-permute-start | bytes 786440 | tf_op jit(solution)/shard_map/ppermute | solution.py:392
  341.8 13.9 %collective-permute-start.5 = (bf16[2,512,128]{2,1,0:T(8,128)(2,1)}, bf16[2,512,128]{2,1,0:T(8,128)(2,1)S(1)}, u32[]{:S(2)}, u32[]{:S(2)}) collective-permute-start(bf16[2,512,128]{2,1,0:T(8,128)(2,1)} %get-tuple-element.57), channel_id=1, source_target_pairs={{0,2},{1,3},{2,4},{3,5},{4,6},{5,7},{8,10},{9,11},{10,12},{11,13},... | collective-permute-start | bytes 786440 | tf_op jit(solution)/shard_map/ppermute | solution.py:399
  345.1 20.7 %collective-permute-start.6 = (bf16[2,512,128]{2,1,0:T(8,128)(2,1)}, bf16[2,512,128]{2,1,0:T(8,128)(2,1)S(1)}, u32[]{:S(2)}, u32[]{:S(2)}) collective-permute-start(bf16[2,512,128]{2,1,0:T(8,128)(2,1)} %get-tuple-element.58), channel_id=1, source_target_pairs={{2,0},{3,1},{4,2},{5,3},{6,4},{7,5},{10,8},{11,9},{12,10},{13,11},... | collective-permute-start | bytes 786440 | tf_op jit(solution)/shard_map/ppermute | solution.py:399
  355.8 10.1 %copy-start.28 = (bf16[2,512,128]{2,1,0:T(8,128)(2,1)}, bf16[2,512,128]{2,1,0:T(8,128)(2,1)S(1)}, u32[]{:S(2)}) copy-start(bf16[2,512,128]{2,1,0:T(8,128)(2,1)S(1)} %collective-permute-done.5.before_ref) | copy-start | bytes 786436
  377.1 10.9 %collective-permute-start.16 = (bf16[2,512,256]{2,1,0:T(8,128)(2,1)S(1)}, bf16[2,512,256]{2,1,0:T(8,128)(2,1)S(1)}, u32[]{:S(2)}, u32[]{:S(2)}) collective-permute-start(bf16[2,512,256]{2,1,0:T(8,128)(2,1)S(1)} %copy-done.18), channel_id=1, source_target_pairs={{0,1},{1,0},{2,3},{3,2},{4,5},{5,4},{6,7},{7,6},{8,9},{9,8},{10,11... | collective-permute-start | bytes 1572872 | tf_op jit(solution)/shard_map/ppermute | solution.py:404
  380.2 10.8 %collective-permute-start.13 = (bf16[2,128,512]{2,1,0:T(8,128)(2,1)}, bf16[2,128,512]{2,1,0:T(8,128)(2,1)S(1)}, u32[]{:S(2)}, u32[]{:S(2)}) collective-permute-start(bf16[2,128,512]{2,1,0:T(8,128)(2,1)} %get-tuple-element.74), channel_id=1, source_target_pairs={{0,8},{8,16},{16,24},{1,9},{9,17},{17,25},{2,10},{10,18},{18,26},{... | collective-permute-start | bytes 786440 | tf_op jit(solution)/shard_map/ppermute | solution.py:392
  382.6 8.5 %collective-permute-start.14 = (bf16[2,128,512]{2,1,0:T(8,128)(2,1)}, bf16[2,128,512]{2,1,0:T(8,128)(2,1)S(1)}, u32[]{:S(2)}, u32[]{:S(2)}) collective-permute-start(bf16[2,128,512]{2,1,0:T(8,128)(2,1)} %get-tuple-element.75), channel_id=1, source_target_pairs={{8,0},{16,8},{24,16},{9,1},{17,9},{25,17},{10,2},{18,10},{26,18},{... | collective-permute-start | bytes 786440 | tf_op jit(solution)/shard_map/ppermute | solution.py:392
  391.1 9.9 %copy-start.32 = (bf16[1,128,512]{2,1,0:T(8,128)(2,1)S(1)}, bf16[1,128,512]{2,1,0:T(8,128)(2,1)}, u32[]{:S(2)}) copy-start(bf16[1,128,512]{2,1,0:T(8,128)(2,1)} %get-tuple-element.82) | copy-start | bytes 393220
  391.1 12.3 %copy-start.31 = (bf16[1,128,512]{2,1,0:T(8,128)(2,1)S(1)}, bf16[1,128,512]{2,1,0:T(8,128)(2,1)}, u32[]{:S(2)}) copy-start(bf16[1,128,512]{2,1,0:T(8,128)(2,1)} %get-tuple-element.83) | copy-start | bytes 393220
  391.1 14.3 %copy-start.17 = (bf16[2,512,256]{2,1,0:T(8,128)(2,1)S(1)}, bf16[2,512,256]{2,1,0:T(8,128)(2,1)}, u32[]{:S(2)}) copy-start(bf16[2,512,256]{2,1,0:T(8,128)(2,1)} %get-tuple-element.90) | copy-start | bytes 1572868
  396.8 17.5 %collective-permute-start.17 = (bf16[2,512,128]{2,1,0:T(8,128)(2,1)}, bf16[2,512,128]{2,1,0:T(8,128)(2,1)S(1)}, u32[]{:S(2)}, u32[]{:S(2)}) collective-permute-start(bf16[2,512,128]{2,1,0:T(8,128)(2,1)} %get-tuple-element.80), channel_id=1, source_target_pairs={{0,2},{1,3},{2,4},{3,5},{4,6},{5,7},{8,10},{9,11},{10,12},{11,13},... | collective-permute-start | bytes 786440 | tf_op jit(solution)/shard_map/ppermute | solution.py:399
  399.7 22.2 %collective-permute-start.18 = (bf16[2,512,128]{2,1,0:T(8,128)(2,1)}, bf16[2,512,128]{2,1,0:T(8,128)(2,1)S(1)}, u32[]{:S(2)}, u32[]{:S(2)}) collective-permute-start(bf16[2,512,128]{2,1,0:T(8,128)(2,1)} %get-tuple-element.81), channel_id=1, source_target_pairs={{2,0},{3,1},{4,2},{5,3},{6,4},{7,5},{10,8},{11,9},{12,10},{13,11},... | collective-permute-start | bytes 786440 | tf_op jit(solution)/shard_map/ppermute | solution.py:399
  401.0 5.5 %collective-permute-start.19 = (bf16[1,128,512]{2,1,0:T(8,128)(2,1)S(1)}, bf16[1,128,512]{2,1,0:T(8,128)(2,1)S(1)}, u32[]{:S(2)}, u32[]{:S(2)}) collective-permute-start(bf16[1,128,512]{2,1,0:T(8,128)(2,1)S(1)} %copy-done.32), channel_id=1, source_target_pairs={{0,8},{8,16},{16,24},{1,9},{9,17},{17,25},{2,10},{10,18},{18,26},{... | collective-permute-start | bytes 393224 | tf_op jit(solution)/shard_map/ppermute | solution.py:392
  403.4 6.7 %collective-permute-start.20 = (bf16[1,128,512]{2,1,0:T(8,128)(2,1)S(1)}, bf16[1,128,512]{2,1,0:T(8,128)(2,1)S(1)}, u32[]{:S(2)}, u32[]{:S(2)}) collective-permute-start(bf16[1,128,512]{2,1,0:T(8,128)(2,1)S(1)} %copy-done.31), channel_id=1, source_target_pairs={{8,0},{16,8},{24,16},{9,1},{17,9},{25,17},{10,2},{18,10},{26,18},{... | collective-permute-start | bytes 393224 | tf_op jit(solution)/shard_map/ppermute | solution.py:392
  405.4 34.5 %collective-permute-start.24 = (bf16[2,512,256]{2,1,0:T(8,128)(2,1)S(1)}, bf16[2,512,256]{2,1,0:T(8,128)(2,1)S(1)}, u32[]{:S(2)}, u32[]{:S(2)}) collective-permute-start(bf16[2,512,256]{2,1,0:T(8,128)(2,1)S(1)} %copy-done.17), channel_id=1, source_target_pairs={{0,1},{1,0},{2,3},{3,2},{4,5},{5,4},{6,7},{7,6},{8,9},{9,8},{10,11... | collective-permute-start | bytes 1572872 | tf_op jit(solution)/shard_map/ppermute | solution.py:404
  414.3 13.9 %copy-start.34 = (bf16[1,512,128]{2,1,0:T(8,128)(2,1)S(1)}, bf16[1,512,128]{2,1,0:T(8,128)(2,1)}, u32[]{:S(2)}) copy-start(bf16[1,512,128]{2,1,0:T(8,128)(2,1)} %get-tuple-element.86) | copy-start | bytes 393220
  414.3 15.2 %copy-start.33 = (bf16[1,512,128]{2,1,0:T(8,128)(2,1)S(1)}, bf16[1,512,128]{2,1,0:T(8,128)(2,1)}, u32[]{:S(2)}) copy-start(bf16[1,512,128]{2,1,0:T(8,128)(2,1)} %get-tuple-element.87) | copy-start | bytes 393220
  414.3 7.6 %copy-start.20 = (bf16[2,512,128]{2,1,0:T(8,128)(2,1)}, bf16[2,512,128]{2,1,0:T(8,128)(2,1)S(1)}, u32[]{:S(2)}) copy-start(bf16[2,512,128]{2,1,0:T(8,128)(2,1)S(1)} %collective-permute-done.17.before_ref) | copy-start | bytes 786436
  427.3 12.6 %collective-permute-start.25 = (bf16[2,512,256]{2,1,0:T(8,128)(2,1)}, bf16[2,512,256]{2,1,0:T(8,128)(2,1)S(1)}, u32[]{:S(2)}, u32[]{:S(2)}) collective-permute-start(bf16[2,512,256]{2,1,0:T(8,128)(2,1)} %get-tuple-element.91), channel_id=1, source_target_pairs={{0,1},{1,0},{2,3},{3,2},{4,5},{5,4},{6,7},{7,6},{8,9},{9,8},{10,11... | collective-permute-start | bytes 1572872 | tf_op jit(solution)/shard_map/ppermute | solution.py:404
  428.2 4.6 collective-permute-start.21
  429.5 6.2 %collective-permute-start.22 = (bf16[1,512,128]{2,1,0:T(8,128)(2,1)S(1)}, bf16[1,512,128]{2,1,0:T(8,128)(2,1)S(1)}, u32[]{:S(2)}, u32[]{:S(2)}) collective-permute-start(bf16[1,512,128]{2,1,0:T(8,128)(2,1)S(1)} %copy-done.33), channel_id=1, source_target_pairs={{2,0},{3,1},{4,2},{5,3},{6,4},{7,5},{10,8},{11,9},{12,10},{13,11},... | collective-permute-start | bytes 393224 | tf_op jit(solution)/shard_map/ppermute | solution.py:399
  440.9 20.2 %copy-start.19 = (bf16[1,512,256]{2,1,0:T(8,128)(2,1)S(1)}, bf16[1,512,256]{2,1,0:T(8,128)(2,1)}, u32[]{:S(2)}) copy-start(bf16[1,512,256]{2,1,0:T(8,128)(2,1)} %get-tuple-element.99) | copy-start | bytes 786436
  443.3 6.8 %collective-permute-start.26 = (bf16[1,128,512]{2,1,0:T(8,128)(2,1)}, bf16[1,128,512]{2,1,0:T(8,128)(2,1)S(1)}, u32[]{:S(2)}, u32[]{:S(2)}) collective-permute-start(bf16[1,128,512]{2,1,0:T(8,128)(2,1)} %get-tuple-element.93), channel_id=1, source_target_pairs={{0,8},{8,16},{16,24},{1,9},{9,17},{17,25},{2,10},{10,18},{18,26},{... | collective-permute-start | bytes 393224 | tf_op jit(solution)/shard_map/ppermute | solution.py:392
  447.8 6.5 %collective-permute-start.27 = (bf16[1,128,512]{2,1,0:T(8,128)(2,1)}, bf16[1,128,512]{2,1,0:T(8,128)(2,1)S(1)}, u32[]{:S(2)}, u32[]{:S(2)}) collective-permute-start(bf16[1,128,512]{2,1,0:T(8,128)(2,1)} %get-tuple-element.94), channel_id=1, source_target_pairs={{8,0},{16,8},{24,16},{9,1},{17,9},{25,17},{10,2},{18,10},{26,18},{... | collective-permute-start | bytes 393224 | tf_op jit(solution)/shard_map/ppermute | solution.py:392
  458.5 4.0 collective-permute-start.28
  459.8 5.9 %collective-permute-start.29 = (bf16[1,512,128]{2,1,0:T(8,128)(2,1)}, bf16[1,512,128]{2,1,0:T(8,128)(2,1)S(1)}, u32[]{:S(2)}, u32[]{:S(2)}) collective-permute-start(bf16[1,512,128]{2,1,0:T(8,128)(2,1)} %get-tuple-element.97), channel_id=1, source_target_pairs={{2,0},{3,1},{4,2},{5,3},{6,4},{7,5},{10,8},{11,9},{12,10},{13,11},... | collective-permute-start | bytes 393224 | tf_op jit(solution)/shard_map/ppermute | solution.py:399
  461.1 10.1 %collective-permute-start.30 = (bf16[1,512,256]{2,1,0:T(8,128)(2,1)S(1)}, bf16[1,512,256]{2,1,0:T(8,128)(2,1)S(1)}, u32[]{:S(2)}, u32[]{:S(2)}) collective-permute-start(bf16[1,512,256]{2,1,0:T(8,128)(2,1)S(1)} %copy-done.19), channel_id=1, source_target_pairs={{0,1},{1,0},{2,3},{3,2},{4,5},{5,4},{6,7},{7,6},{8,9},{9,8},{10,11... | collective-permute-start | bytes 786440 | tf_op jit(solution)/shard_map/ppermute | solution.py:404
  469.9 7.0 %collective-permute-start.31 = (bf16[1,512,256]{2,1,0:T(8,128)(2,1)}, bf16[1,512,256]{2,1,0:T(8,128)(2,1)S(1)}, u32[]{:S(2)}, u32[]{:S(2)}) collective-permute-start(bf16[1,512,256]{2,1,0:T(8,128)(2,1)} %get-tuple-element.100), channel_id=1, source_target_pairs={{0,1},{1,0},{2,3},{3,2},{4,5},{5,4},{6,7},{7,6},{8,9},{9,8},{10,11... | collective-permute-start | bytes 786440 | tf_op jit(solution)/shard_map/ppermute | solution.py:404
  (30 other events, 62.0 us)
Sparse Core Ops, SparseCore 0:
  18.7 146.3 reduce-scatter.5
  167.4 77.6 reduce-scatter.7
  247.5 83.1 reduce-scatter.9
  332.9 49.5 reduce-scatter.11
  384.7 50.3 reduce-scatter.13

commit v3 on v2

--- a/solution.py
+++ b/solution.py
@@ -23,7 +23,7 @@
     return chunks
 
 
-VMEM = 60 * 1024 * 1024
+VMEM = 64 * 1024 * 1024
 
 
 def params():
@@ -268,41 +268,43 @@
     )(place, bounded, before, after, tiles_y, labels, *behind)
 
 
-def join_planes(kept, came, perm_back, slots_of, planes, rows):
+def join_planes(kept, came, perm_back, slots_of, planes, kernels, kernel_id, rows, base=()):
     _, slab_x, narrow = kept[0].shape
     span = perm_back.shape[0]
     sub = span // planes
     half = planes // PAIR
-    kernels = len(slots_of) // half
     count = len(kept)
 
     def body(*refs):
         kept_refs, came_refs = refs[:count], refs[count : 2 * count]
-        perm_ref, out_ref, stack_ref = refs[2 * count :]
-        for k in range(kernels):
-            for b in range(rows // sub):
-                for j in range(half):
-                    c, m = slots_of[k * half + j]
-                    at = slice(b * sub, (b + 1) * sub)
-                    stack_ref[j * sub : (j + 1) * sub] = kept_refs[c][m, at]
-                    stack_ref[(half + j) * sub : (half + j + 1) * sub] = came_refs[c][m, at]
-                moved = jnp.dot(perm_ref[...], stack_ref[...], preferred_element_type=jnp.float32)
-                moved = moved.reshape(sub, planes, narrow).astype(jnp.bfloat16)
-                out_ref[b * sub : (b + 1) * sub, k] = moved
+        perm_ref = refs[2 * count]
+        out_ref, stack_ref = refs[-2:]
+        for b in range(rows // sub):
+            at = slice(b * sub, (b + 1) * sub)
+            for j in range(half):
+                c, m = slots_of[j]
+                stack_ref[j * sub : (j + 1) * sub] = kept_refs[c][m, at]
+                stack_ref[(half + j) * sub : (half + j + 1) * sub] = came_refs[c][m, at]
+            moved = jnp.dot(perm_ref[...], stack_ref[...], preferred_element_type=jnp.float32)
+            out_ref[at, 0] = moved.reshape(sub, planes, narrow).astype(jnp.bfloat16)
 
     specs = [pl.BlockSpec((a.shape[0], rows, narrow), lambda i: (0, i, 0)) for a in kept]
-    size = slab_x * kernels * planes * narrow
+    size = slab_x * planes * narrow
     return pl.pallas_call(
         body,
         grid=(slab_x // rows,),
-        in_specs=specs + specs + [pl.BlockSpec(perm_back.shape, lambda i: (0, 0))],
-        out_specs=pl.BlockSpec((rows, kernels, planes, narrow), lambda i: (i, 0, 0, 0)),
+        in_specs=specs
+        + specs
+        + [pl.BlockSpec(perm_back.shape, lambda i: (0, 0))]
+        + [pl.BlockSpec(memory_space=pl.ANY)] * len(base),
+        out_specs=pl.BlockSpec((rows, 1, planes, narrow), lambda i: (i, kernel_id, 0, 0)),
         out_shape=jax.ShapeDtypeStruct((slab_x, kernels, planes, narrow), jnp.bfloat16),
         scratch_shapes=[pltpu.VMEM((span, narrow), jnp.bfloat16)],
+        input_output_aliases={2 * count + 1: 0} if base else {},
         compiler_params=params(),
         cost_estimate=cost(2 * span * size, 4 * size),
         name="join_planes",
-    )(*kept, *came, perm_back)
+    )(*kept, *came, perm_back, *base)
 
 
 def per_device(partial_kernels, illumination, classes_x, classes_y, widths_x, widths_y):
@@ -426,8 +428,14 @@
         divide(n, [kept[n - 1], came[0], came[2]])
         cross_x(n)
         cross_y(n)
-    order = range(last)
-    return join_planes([kept[n] for n in order], [came[n] for n in order], perm.T, slots_of, planes, slab_x // 2)
+    base = ()
+    for k in range(kernels):
+        mine = [n for n in range(last) if chunks[n][1] == k]
+        where = [slots_of[k * half + j] for j in range(half)]
+        where = [(mine.index(n), m) for n, m in where]
+        parts = [kept[n] for n in mine], [came[n] for n in mine]
+        base = (join_planes(*parts, perm.T, where, planes, kernels, k, slab_x // 2, base),)
+    return base[0]
 
 
 def solution(mesh):

time: 490 us -> 486 us (level)
  local copies, waits for them, and re-layouts: 23.9 us -> 15 us
  waiting for transfers between devices: 260 us -> 252 us
  starting transfers between devices: 61.7 us -> 69.2 us
    unnamed x84 -> x8, local copies, waits for them, and re-layouts: 14.2 us -> 2.85 us
    ppermute x10, starting transfers between devices: 18.6 us -> 25.6 us  [cross_x(): ends[n] = (lax.ppermute(high, 'ev', z_up), lax.ppermute(low, 'ev', z_down))]
  transfers between devices with their start and end apart: 37 -> 37, of which waited for: 21 -> 22; matrix products, arithmetic and copies ran while one was open for 4% -> 5% of each run, Pallas kernels for 20% -> 21%
where the time goes in v3:
time: 486 us; the launch traced here: 484 us
  waiting for transfers between devices  252 us (52%)
  Pallas kernels  123 us (25%)
  starting transfers between devices  69.2 us (14%)
  local copies, waits for them, and re-layouts  15 us (3%)
  between operations  13.4 us (3%)
  other arithmetic  11.9 us (2%)
    ppermute x4, waiting for transfers between devices, begin(): added[n] = add_parts(own, lax.ppermute(sent, 'ev', other), after)  146 us
    ppermute x10, waiting for transfers between devices, cross_x(): ends[n] = (lax.ppermute(high, 'ev', z_up), lax.ppermute(low, 'ev', z_down))  51.1 us
    pallas_call x3, Pallas kernels, split_planes(): pl.pallas_call(body, grid=(shards, slab_x // rows), in_specs=[pl.BlockSpe...  35.5 us
    ppermute x10, starting transfers between devices, cross_x(): ends[n] = (lax.ppermute(high, 'ev', z_up), lax.ppermute(low, 'ev', z_down))  25.6 us
    pallas_call x4, Pallas kernels, add_parts(): pl.pallas_call(body, grid=(shards, slots), in_specs=[spec, spec] + [pl.Bl...  24.4 us
    ppermute x5, starting transfers between devices, divide(): lax.ppermute(bottom, 'gx', x_up)  21.9 us
    pallas_call x5, Pallas kernels, smooth_x(): pl.pallas_call(body, grid=(slots,), in_specs=[full, edge, edge, pl.BlockS...  21.7 us
    pallas_call x5, Pallas kernels, smooth_y(): pl.pallas_call(body, grid_spec=pltpu.PrefetchScalarGridSpec(num_scalar_pr...  21 us
  transfers between devices with their start and end apart: 37, of which 22 were waited for; matrix products, arithmetic and copies ran while one was open for 5% of the time, Pallas kernels for 21%

profile of v3, /device:TPU:1, one launch (start us, length us, event | category | flops | bytes accessed | tf_op | source)
XLA Modules:
  0.0 484.4 jit_solution(4884903629017089986)
XLA Ops:
  7.5 11.1 %split_planes.3.refs_0_ = bf16[4,4,512,512]{3,2,1,0:T(8,128)(2,1)} custom-call(bf16[1,512,2,8,2048]{4,3,2,1,0:T(8,128)(2,1)} %part_ref.5, bf16[256,256]{1,0:T(8,128)(2,1)} %get-tuple-element.106.perm_ref), custom_call_target="tpu_custom_call" | custom-call | tf_op jit(solution)/shard_map/split_planes/pallas_call | solution.py:63
  25.0 11.3 %split_planes.4 = (bf16[4,2,512,512]{3,2,1,0:T(8,128)(2,1)}, bf16[4,2,512,512]{3,2,1,0:T(8,128)(2,1)}) custom-call(bf16[1,512,2,8,2048]{4,3,2,1,0:T(8,128)(2,1)} %part_ref.5, bf16[256,256]{1,0:T(8,128)(2,1)} %get-tuple-element.106.perm_ref, bf16[4,4,512,512]{3,2,1,0:T(8,128)(2,1)} %split_planes.3.refs_0_), custom_call_target="tpu_custom_call" | custom-call | tf_op jit(solution)/shard_map/split_planes/pallas_call | solution.py:63
  36.4 11.3 %collective-permute-done.4.refs_2_ = s32[4,256]{1,0:T(4,128)} collective-permute-done((s32[4,256]{1,0:T(4,128)}, s32[4,256]{1,0:T(4,128)}, u32[]{:S(2)}, u32[]{:S(2)}) %collective-permute-start.4) | collective-permute-done | bytes 4128 | tf_op jit(solution)/shard_map/ppermute | solution.py:360
  48.9 13.1 %split_planes.5 = (bf16[4,2,512,512]{3,2,1,0:T(8,128)(2,1)}, bf16[4,2,512,512]{3,2,1,0:T(8,128)(2,1)}, bf16[4,1,512,512]{3,2,1,0:T(8,128)(2,1)}, bf16[4,1,512,51...) custom-call(bf16[1,512,2,8,2048]{4,3,2,1,0:T(8,128)(2,1)} %part_ref.5, ...), custom_call_target="tpu_custom_call" | custom-call | tf_op jit(solution)/shard_map/split_planes/pallas_call | solution.py:63
  61.9 76.9 %collective-permute-done.6.b_ref = bf16[4,2,512,512]{3,2,1,0:T(8,128)(2,1)} collective-permute-done((bf16[4,2,512,512]{3,2,1,0:T(8,128)(2,1)}, bf16[4,2,512,512]{3,2,1,0:T(8,128)(2,1)}, u32[]{:S(2)}, u32[]{:S(2)}) %collective-permute-start.6) | collective-permute-done | bytes 4194336 | tf_op jit(solution)/shard_map/ppermute | solution.py:383
  138.9 7.9 %add_parts.5 = bf16[4,2,512,512]{3,2,1,0:T(8,128)(2,1)} custom-call(bf16[4,2,512,512]{3,2,1,0:T(8,128)(2,1)} %get-tuple-element.53.refs_0_.a_ref, bf16[4,2,512,512]{3,2,1,0:T(8,128)(2,1)} %collective-permute-done.6.b_ref, bf16[4,2,512,512]{3,2,1,0:T(8,128)(2,1)} %get-tuple-element.54.a_ref.refs_0_, bf16[4,1,512,512]{3,2,1,0:T(8,128)(2,1)} %get-tuple-element.59.refs_1_.a_ref, ...), custom_call_target="tpu_custom_call" | custom-call | flops 2097152 | bytes 12582912 | tf_op jit(solution)/shard_map/add_parts/pallas_call | solution.py:104
  147.6 17.5 %reduce-scatter.6.cloned.1.call-done = bf16[1,4,512,512]{3,2,1,0:T(8,128)(2,1)} async-done(((bf16[4,4,512,512]{3,2,1,0:T(8,128)(2,1)}), bf16[1,4,512,512]{3,2,1,0:T(8,128)(2,1)}) %reduce-scatter.6.cloned.1.call-update) | async-done | bytes 2097168 | tf_op jit(solution)/shard_map/reduce_scatter | solution.py:331
  165.1 3.0 slice_bitcast_fusion
  168.1 69.0 %collective-permute-done.b_ref = bf16[4,2,512,512]{3,2,1,0:T(8,128)(2,1)} collective-permute-done((bf16[4,2,512,512]{3,2,1,0:T(8,128)(2,1)}, bf16[4,2,512,512]{3,2,1,0:T(8,128)(2,1)}, u32[]{:S(2)}, u32[]{:S(2)}) %collective-permute-start) | collective-permute-done | bytes 4194336 | tf_op jit(solution)/shard_map/ppermute | solution.py:383
  237.2 7.9 %add_parts.4 = bf16[4,2,512,512]{3,2,1,0:T(8,128)(2,1)} custom-call(bf16[4,2,512,512]{3,2,1,0:T(8,128)(2,1)} %get-tuple-element.54.a_ref.refs_0_, bf16[4,2,512,512]{3,2,1,0:T(8,128)(2,1)} %collective-permute-done.b_ref, bf16[2,512,512]{2,1,0:T(8,128)(2,1)} %get-tuple-element.102.refs_0_), custom_call_target="tpu_custom_call" | custom-call | flops 2097152 | bytes 12582912 | tf_op jit(solution)/shard_map/add_parts/pallas_call | solution.py:104
  250.9 3.2 add_convert_fusion.tiles_ref
  254.0 3.4 scale.6
  257.4 6.2 %collective-permute-start.7 = (bf16[2,128,512]{2,1,0:T(8,128)(2,1)}, bf16[2,128,512]{2,1,0:T(8,128)(2,1)}, u32[]{:S(2)}, u32[]{:S(2)}) collective-permute-start(bf16[2,128,512]{2,1,0:T(8,128)(2,1)} %get-tuple-element.64), channel_id=1, source_target_pairs={{0,8},{8,16},{16,24},{1,9},{9,17},{17,25},{2,10},{10,18},{18,26},{... | collective-permute-start | bytes 786440 | tf_op jit(solution)/shard_map/ppermute | solution.py:394
  265.5 2.9 fusion.9
  271.9 5.0 %smooth_x.5 = (bf16[2,512,512]{2,1,0:T(8,128)(2,1)}, bf16[2,512,128]{2,1,0:T(8,128)(2,1)}, bf16[2,512,128]{2,1,0:T(8,128)(2,1)}) custom-call(bf16[2,512,512]{2,1,0:T(8,128)(2,1)} %get-tuple-element.63.mid_ref, bf16[2,128,512]{2,1,0:T(8,128)(2,1)} %collective-permute-done.7.before_ref, bf16[2,128,512]{2,1,0:T(8,128)(2,1)} %collective-permute-done.8.after_ref, ...), custom_call_target="tpu_custom_call" | custom-call | flops 1610612736 | bytes 3145728 | tf_op jit(solution)/shard_map/smooth_x/pallas_call | solution.py:197
  276.9 3.9 collective-permute-start.9
  282.6 3.2 fusion.16.tiles_ref
  287.8 3.6 collective-permute-done.9.before_ref
  291.5 10.8 %collective-permute-done.10.after_ref = bf16[2,512,128]{2,1,0:T(8,128)(2,1)} collective-permute-done((bf16[2,512,128]{2,1,0:T(8,128)(2,1)}, bf16[2,512,128]{2,1,0:T(8,128)(2,1)}, u32[]{:S(2)}, u32[]{:S(2)}) %collective-permute-start.10) | collective-permute-done | bytes 262176 | tf_op jit(solution)/shard_map/ppermute | solution.py:401
  302.2 4.7 smooth_y.5
  306.9 5.2 %collective-permute-done.11.refs_1_ = bf16[2,512,512]{2,1,0:T(8,128)(2,1)} collective-permute-done((bf16[2,512,512]{2,1,0:T(8,128)(2,1)}, bf16[2,512,512]{2,1,0:T(8,128)(2,1)}, u32[]{:S(2)}, u32[]{:S(2)}) %collective-permute-start.11) | collective-permute-done | bytes 1048608 | tf_op jit(solution)/shard_map/ppermute | solution.py:387
  312.1 4.3 add_parts.6
  316.5 3.2 scale.8
  319.7 7.4 %collective-permute-start.20 = (bf16[2,128,512]{2,1,0:T(8,128)(2,1)}, bf16[2,128,512]{2,1,0:T(8,128)(2,1)}, u32[]{:S(2)}, u32[]{:S(2)}) collective-permute-start(bf16[2,128,512]{2,1,0:T(8,128)(2,1)} %get-tuple-element.84), channel_id=1, source_target_pairs={{0,8},{8,16},{16,24},{1,9},{9,17},{17,25},{2,10},{10,18},{18,26},{... | collective-permute-start | bytes 786440 | tf_op jit(solution)/shard_map/ppermute | solution.py:394
  330.7 4.7 collective-permute-done.21.after_ref
  335.4 4.8 smooth_x.8
  340.2 3.9 collective-permute-start.22
  345.4 8.6 %collective-permute-done.22.before_ref = bf16[2,512,128]{2,1,0:T(8,128)(2,1)} collective-permute-done((bf16[2,512,128]{2,1,0:T(8,128)(2,1)}, bf16[2,512,128]{2,1,0:T(8,128)(2,1)}, u32[]{:S(2)}, u32[]{:S(2)}) %collective-permute-start.22) | collective-permute-done | bytes 262176 | tf_op jit(solution)/shard_map/ppermute | solution.py:401
  354.0 11.1 %collective-permute-done.23.after_ref = bf16[2,512,128]{2,1,0:T(8,128)(2,1)} collective-permute-done((bf16[2,512,128]{2,1,0:T(8,128)(2,1)}, bf16[2,512,128]{2,1,0:T(8,128)(2,1)}, u32[]{:S(2)}, u32[]{:S(2)}) %collective-permute-start.23) | collective-permute-done | bytes 262176 | tf_op jit(solution)/shard_map/ppermute | solution.py:401
  365.1 4.7 smooth_y.8
  369.8 4.3 add_parts.7
  387.5 4.8 smooth_x.6
  392.3 3.7 collective-permute-start.13
  399.3 2.9 collective-permute-start.16
  406.2 3.5 smooth_x.7
  409.7 7.3 %collective-permute-done.14.after_ref = bf16[2,512,128]{2,1,0:T(8,128)(2,1)} collective-permute-done((bf16[2,512,128]{2,1,0:T(8,128)(2,1)}, bf16[2,512,128]{2,1,0:T(8,128)(2,1)}, u32[]{:S(2)}, u32[]{:S(2)}) %collective-permute-start.14) | collective-permute-done | bytes 262176 | tf_op jit(solution)/shard_map/ppermute | solution.py:401
  417.0 4.7 smooth_y.6
  427.0 4.5 collective-permute-done.17.before_ref
  433.2 3.5 smooth_y.7
  439.0 3.8 collective-permute-start.26
  445.1 4.4 collective-permute-done.27.after_ref
  449.5 3.5 smooth_x.9
  453.0 4.9 %collective-permute-start.28 = (bf16[1,512,128]{2,1,0:T(8,128)(2,1)}, bf16[1,512,128]{2,1,0:T(8,128)(2,1)}, u32[]{:S(2)}, u32[]{:S(2)}) collective-permute-start(bf16[1,512,128]{2,1,0:T(8,128)(2,1)} %get-tuple-element.96), channel_id=1, source_target_pairs={{0,2},{1,3},{2,4},{3,5},{4,6},{5,7},{8,10},{9,11},{10,12},{11,13},... | collective-permute-start | bytes 393224 | tf_op jit(solution)/shard_map/ppermute | solution.py:401
  460.5 3.5 collective-permute-done.29.after_ref
  464.0 3.5 smooth_y.9
  468.7 3.1 join_planes.2.refs_7_
  471.8 2.9 collective-permute-done.31.refs_5_
  474.7 3.2 join_planes.3
  (84 shorter events, 65.3 us)
Async XLA Ops:
  6.5 158.6 %reduce-scatter.6.cloned.1.call-start = ((), (), s32[]{:S(2)}) async-start(), calls=%async_computation.5 | async-start | bytes 10485760 | tf_op jit(solution)/shard_map/reduce_scatter | solution.py:331
  18.6 5.9 %copy-start = (s32[8,256]{1,0:T(8,128)S(1)}, s32[8,256]{1,0:T(8,128)}, u32[]{:S(2)}) copy-start(s32[8,256]{1,0:T(8,128)} %param.8) | copy-start | bytes 24580
  18.6 235.4 %reduce-scatter.10.cloned.1.call-start = ((), (), s32[]{:S(2)}) async-start(), calls=%async_computation.7 | async-start | bytes 5242880 | tf_op jit(solution)/shard_map/reduce_scatter | solution.py:331
  22.3 25.4 %collective-permute-start.1 = (bf16[4,512,256]{2,1,0:T(8,128)(2,1)}, bf16[4,512,256]{2,1,0:T(8,128)(2,1)}, u32[]{:S(2)}, u32[]{:S(2)}) collective-permute-start(bf16[4,512,256]{2,1,0:T(8,128)(2,1)} %bitcast.18), channel_id=1, source_target_pairs={{0,1},{1,0},{2,3},{3,2},{4,5},{5,4},{6,7},{7,6},{8,9},{9,8},{10,11... | collective-permute-start | bytes 3145736 | tf_op jit(solution)/shard_map/ppermute | solution.py:347
  25.0 22.7 %collective-permute-start.4 = (s32[4,256]{1,0:T(4,128)}, s32[4,256]{1,0:T(4,128)}, u32[]{:S(2)}, u32[]{:S(2)}) collective-permute-start(s32[4,256]{1,0:T(4,128)} %get-tuple-element.104), channel_id=1, source_target_pairs={{0,1},{1,0},{2,3},{3,2},{4,5},{5,4},{6,7},{7,6},{8,9},{9,8},{10,11... | collective-permute-start | bytes 12296 | tf_op jit(solution)/shard_map/ppermute | solution.py:360
  47.7 91.2 %collective-permute-start.6 = (bf16[4,2,512,512]{3,2,1,0:T(8,128)(2,1)}, bf16[4,2,512,512]{3,2,1,0:T(8,128)(2,1)}, u32[]{:S(2)}, u32[]{:S(2)}) collective-permute-start(bf16[4,2,512,512]{3,2,1,0:T(8,128)(2,1)} %hold.1), channel_id=1, source_target_pairs={{0,1},{1,0},{2,3},{3,2},{4,5},{5,4},{6,7},{7,6},{8,9},{9,8},{10,11... | collective-permute-start | bytes 12582920 | tf_op jit(solution)/shard_map/ppermute | solution.py:383
  146.8 227.4 %reduce-scatter.8.cloned.1.call-start = ((), (), s32[]{:S(2)}) async-start(), calls=%async_computation.6 | async-start | bytes 5242880 | tf_op jit(solution)/shard_map/reduce_scatter | solution.py:331
  146.8 90.3 %collective-permute-start = (bf16[4,2,512,512]{3,2,1,0:T(8,128)(2,1)}, bf16[4,2,512,512]{3,2,1,0:T(8,128)(2,1)}, u32[]{:S(2)}, u32[]{:S(2)}) collective-permute-start(bf16[4,2,512,512]{3,2,1,0:T(8,128)(2,1)} %get-tuple-element.55), channel_id=1, source_target_pairs={{0,1},{1,0},{2,3},{3,2},{4,5},{5,4},{6,7},{7,6},{8,9},{9,8},{10,11... | collective-permute-start | bytes 12582920 | tf_op jit(solution)/shard_map/ppermute | solution.py:383
  245.0 138.8 %reduce-scatter.12.cloned.1.call-start = ((), (), s32[]{:S(2)}) async-start(), calls=%async_computation.8 | async-start | bytes 2621440 | tf_op jit(solution)/shard_map/reduce_scatter | solution.py:331
  245.1 61.8 %collective-permute-start.5 = (bf16[4,1,512,512]{3,2,1,0:T(8,128)(2,1)}, bf16[4,1,512,512]{3,2,1,0:T(8,128)(2,1)}, u32[]{:S(2)}, u32[]{:S(2)}) collective-permute-start(bf16[4,1,512,512]{3,2,1,0:T(8,128)(2,1)} %get-tuple-element.60), channel_id=1, source_target_pairs={{0,1},{1,0},{2,3},{3,2},{4,5},{5,4},{6,7},{7,6},{8,9},{9,8},{10,11... | collective-permute-start | bytes 6291464 | tf_op jit(solution)/shard_map/ppermute | solution.py:383
  247.9 2.3 copy-start.1
  247.9 2.3 copy-start.2
  257.4 13.0 %collective-permute-start.7 = (bf16[2,128,512]{2,1,0:T(8,128)(2,1)}, bf16[2,128,512]{2,1,0:T(8,128)(2,1)}, u32[]{:S(2)}, u32[]{:S(2)}) collective-permute-start(bf16[2,128,512]{2,1,0:T(8,128)(2,1)} %get-tuple-element.64), channel_id=1, source_target_pairs={{0,8},{8,16},{16,24},{1,9},{9,17},{17,25},{2,10},{10,18},{18,26},{... | collective-permute-start | bytes 786440 | tf_op jit(solution)/shard_map/ppermute | solution.py:394
  263.6 8.3 %collective-permute-start.8 = (bf16[2,128,512]{2,1,0:T(8,128)(2,1)}, bf16[2,128,512]{2,1,0:T(8,128)(2,1)}, u32[]{:S(2)}, u32[]{:S(2)}) collective-permute-start(bf16[2,128,512]{2,1,0:T(8,128)(2,1)} %get-tuple-element.65), channel_id=1, source_target_pairs={{8,0},{16,8},{24,16},{9,1},{17,9},{25,17},{10,2},{18,10},{26,18},{... | collective-permute-start | bytes 786440 | tf_op jit(solution)/shard_map/ppermute | solution.py:394
  276.9 14.6 %collective-permute-start.9 = (bf16[2,512,128]{2,1,0:T(8,128)(2,1)}, bf16[2,512,128]{2,1,0:T(8,128)(2,1)}, u32[]{:S(2)}, u32[]{:S(2)}) collective-permute-start(bf16[2,512,128]{2,1,0:T(8,128)(2,1)} %get-tuple-element.67), channel_id=1, source_target_pairs={{0,2},{1,3},{2,4},{3,5},{4,6},{5,7},{8,10},{9,11},{10,12},{11,13},... | collective-permute-start | bytes 786440 | tf_op jit(solution)/shard_map/ppermute | solution.py:401
  280.8 21.4 %collective-permute-start.10 = (bf16[2,512,128]{2,1,0:T(8,128)(2,1)}, bf16[2,512,128]{2,1,0:T(8,128)(2,1)}, u32[]{:S(2)}, u32[]{:S(2)}) collective-permute-start(bf16[2,512,128]{2,1,0:T(8,128)(2,1)} %get-tuple-element.68), channel_id=1, source_target_pairs={{2,0},{3,1},{4,2},{5,3},{6,4},{7,5},{10,8},{11,9},{12,10},{13,11},... | collective-permute-start | bytes 786440 | tf_op jit(solution)/shard_map/ppermute | solution.py:401
  282.3 29.8 %collective-permute-start.11 = (bf16[2,512,512]{2,1,0:T(8,128)(2,1)}, bf16[2,512,512]{2,1,0:T(8,128)(2,1)}, u32[]{:S(2)}, u32[]{:S(2)}) collective-permute-start(bf16[2,512,512]{2,1,0:T(8,128)(2,1)} %get-tuple-element.101), channel_id=1, source_target_pairs={{0,1},{1,0},{2,3},{3,2},{4,5},{5,4},{6,7},{7,6},{8,9},{9,8},{10,11... | collective-permute-start | bytes 3145736 | tf_op jit(solution)/shard_map/ppermute | solution.py:387
  316.4 120.3 %reduce-scatter.14.cloned.1.call-start = ((), (), s32[]{:S(2)}) async-start(), calls=%async_computation.9 | async-start | bytes 2621440 | tf_op jit(solution)/shard_map/reduce_scatter | solution.py:331
  316.5 53.3 %collective-permute-start.19 = (bf16[4,1,512,512]{3,2,1,0:T(8,128)(2,1)}, bf16[4,1,512,512]{3,2,1,0:T(8,128)(2,1)}, u32[]{:S(2)}, u32[]{:S(2)}) collective-permute-start(bf16[4,1,512,512]{3,2,1,0:T(8,128)(2,1)} %get-tuple-element.82), channel_id=1, source_target_pairs={{0,1},{1,0},{2,3},{3,2},{4,5},{5,4},{6,7},{7,6},{8,9},{9,8},{10,11... | collective-permute-start | bytes 6291464 | tf_op jit(solution)/shard_map/ppermute | solution.py:383
  319.7 11.0 %collective-permute-start.20 = (bf16[2,128,512]{2,1,0:T(8,128)(2,1)}, bf16[2,128,512]{2,1,0:T(8,128)(2,1)}, u32[]{:S(2)}, u32[]{:S(2)}) collective-permute-start(bf16[2,128,512]{2,1,0:T(8,128)(2,1)} %get-tuple-element.84), channel_id=1, source_target_pairs={{0,8},{8,16},{16,24},{1,9},{9,17},{17,25},{2,10},{10,18},{18,26},{... | collective-permute-start | bytes 786440 | tf_op jit(solution)/shard_map/ppermute | solution.py:394
  327.1 8.3 %collective-permute-start.21 = (bf16[2,128,512]{2,1,0:T(8,128)(2,1)}, bf16[2,128,512]{2,1,0:T(8,128)(2,1)}, u32[]{:S(2)}, u32[]{:S(2)}) collective-permute-start(bf16[2,128,512]{2,1,0:T(8,128)(2,1)} %get-tuple-element.85), channel_id=1, source_target_pairs={{8,0},{16,8},{24,16},{9,1},{17,9},{25,17},{10,2},{18,10},{26,18},{... | collective-permute-start | bytes 786440 | tf_op jit(solution)/shard_map/ppermute | solution.py:394
  340.2 13.8 %collective-permute-start.22 = (bf16[2,512,128]{2,1,0:T(8,128)(2,1)}, bf16[2,512,128]{2,1,0:T(8,128)(2,1)}, u32[]{:S(2)}, u32[]{:S(2)}) collective-permute-start(bf16[2,512,128]{2,1,0:T(8,128)(2,1)} %get-tuple-element.87), channel_id=1, source_target_pairs={{0,2},{1,3},{2,4},{3,5},{4,6},{5,7},{8,10},{9,11},{10,12},{11,13},... | collective-permute-start | bytes 786440 | tf_op jit(solution)/shard_map/ppermute | solution.py:401
  344.1 20.9 %collective-permute-start.23 = (bf16[2,512,128]{2,1,0:T(8,128)(2,1)}, bf16[2,512,128]{2,1,0:T(8,128)(2,1)}, u32[]{:S(2)}, u32[]{:S(2)}) collective-permute-start(bf16[2,512,128]{2,1,0:T(8,128)(2,1)} %get-tuple-element.88), channel_id=1, source_target_pairs={{2,0},{3,1},{4,2},{5,3},{6,4},{7,5},{10,8},{11,9},{12,10},{13,11},... | collective-permute-start | bytes 786440 | tf_op jit(solution)/shard_map/ppermute | solution.py:401
  374.1 9.7 %collective-permute-start.12 = (bf16[2,512,256]{2,1,0:T(8,128)(2,1)}, bf16[2,512,256]{2,1,0:T(8,128)(2,1)}, u32[]{:S(2)}, u32[]{:S(2)}) collective-permute-start(bf16[2,512,256]{2,1,0:T(8,128)(2,1)} %get-tuple-element.70), channel_id=1, source_target_pairs={{0,1},{1,0},{2,3},{3,2},{4,5},{5,4},{6,7},{7,6},{8,9},{9,8},{10,11... | collective-permute-start | bytes 1572872 | tf_op jit(solution)/shard_map/ppermute | solution.py:406
  377.0 9.2 %collective-permute-start.2 = (bf16[2,128,512]{2,1,0:T(8,128)(2,1)}, bf16[2,128,512]{2,1,0:T(8,128)(2,1)}, u32[]{:S(2)}, u32[]{:S(2)}) collective-permute-start(bf16[2,128,512]{2,1,0:T(8,128)(2,1)} %get-tuple-element.57), channel_id=1, source_target_pairs={{0,8},{8,16},{16,24},{1,9},{9,17},{17,25},{2,10},{10,18},{18,26},{... | collective-permute-start | bytes 786440 | tf_op jit(solution)/shard_map/ppermute | solution.py:394
  379.5 8.0 %collective-permute-start.3 = (bf16[2,128,512]{2,1,0:T(8,128)(2,1)}, bf16[2,128,512]{2,1,0:T(8,128)(2,1)}, u32[]{:S(2)}, u32[]{:S(2)}) collective-permute-start(bf16[2,128,512]{2,1,0:T(8,128)(2,1)} %get-tuple-element.58), channel_id=1, source_target_pairs={{8,0},{16,8},{24,16},{9,1},{17,9},{25,17},{10,2},{18,10},{26,18},{... | collective-permute-start | bytes 786440 | tf_op jit(solution)/shard_map/ppermute | solution.py:394
  392.3 17.4 %collective-permute-start.13 = (bf16[2,512,128]{2,1,0:T(8,128)(2,1)}, bf16[2,512,128]{2,1,0:T(8,128)(2,1)}, u32[]{:S(2)}, u32[]{:S(2)}) collective-permute-start(bf16[2,512,128]{2,1,0:T(8,128)(2,1)} %get-tuple-element.73), channel_id=1, source_target_pairs={{0,2},{1,3},{2,4},{3,5},{4,6},{5,7},{8,10},{9,11},{10,12},{11,13},... | collective-permute-start | bytes 786440 | tf_op jit(solution)/shard_map/ppermute | solution.py:401
  396.0 21.0 %collective-permute-start.14 = (bf16[2,512,128]{2,1,0:T(8,128)(2,1)}, bf16[2,512,128]{2,1,0:T(8,128)(2,1)}, u32[]{:S(2)}, u32[]{:S(2)}) collective-permute-start(bf16[2,512,128]{2,1,0:T(8,128)(2,1)} %get-tuple-element.74), channel_id=1, source_target_pairs={{2,0},{3,1},{4,2},{5,3},{6,4},{7,5},{10,8},{11,9},{12,10},{13,11},... | collective-permute-start | bytes 786440 | tf_op jit(solution)/shard_map/ppermute | solution.py:401
  397.3 6.7 %collective-permute-start.15 = (bf16[1,128,512]{2,1,0:T(8,128)(2,1)}, bf16[1,128,512]{2,1,0:T(8,128)(2,1)}, u32[]{:S(2)}, u32[]{:S(2)}) collective-permute-start(bf16[1,128,512]{2,1,0:T(8,128)(2,1)} %get-tuple-element.75), channel_id=1, source_target_pairs={{0,8},{8,16},{16,24},{1,9},{9,17},{17,25},{2,10},{10,18},{18,26},{... | collective-permute-start | bytes 393224 | tf_op jit(solution)/shard_map/ppermute | solution.py:394
  399.3 6.9 %collective-permute-start.16 = (bf16[1,128,512]{2,1,0:T(8,128)(2,1)}, bf16[1,128,512]{2,1,0:T(8,128)(2,1)}, u32[]{:S(2)}, u32[]{:S(2)}) collective-permute-start(bf16[1,128,512]{2,1,0:T(8,128)(2,1)} %get-tuple-element.76), channel_id=1, source_target_pairs={{8,0},{16,8},{24,16},{9,1},{17,9},{25,17},{10,2},{18,10},{26,18},{... | collective-permute-start | bytes 393224 | tf_op jit(solution)/shard_map/ppermute | solution.py:394
  402.2 34.4 %collective-permute-start.24 = (bf16[2,512,256]{2,1,0:T(8,128)(2,1)}, bf16[2,512,256]{2,1,0:T(8,128)(2,1)}, u32[]{:S(2)}, u32[]{:S(2)}) collective-permute-start(bf16[2,512,256]{2,1,0:T(8,128)(2,1)} %get-tuple-element.90), channel_id=1, source_target_pairs={{0,1},{1,0},{2,3},{3,2},{4,5},{5,4},{6,7},{7,6},{8,9},{9,8},{10,11... | collective-permute-start | bytes 1572872 | tf_op jit(solution)/shard_map/ppermute | solution.py:406
  421.7 15.0 %collective-permute-start.25 = (bf16[2,512,256]{2,1,0:T(8,128)(2,1)}, bf16[2,512,256]{2,1,0:T(8,128)(2,1)}, u32[]{:S(2)}, u32[]{:S(2)}) collective-permute-start(bf16[2,512,256]{2,1,0:T(8,128)(2,1)} %get-tuple-element.91), channel_id=1, source_target_pairs={{0,1},{1,0},{2,3},{3,2},{4,5},{5,4},{6,7},{7,6},{8,9},{9,8},{10,11... | collective-permute-start | bytes 1572872 | tf_op jit(solution)/shard_map/ppermute | solution.py:406
  423.1 8.4 %collective-permute-start.17 = (bf16[1,512,128]{2,1,0:T(8,128)(2,1)}, bf16[1,512,128]{2,1,0:T(8,128)(2,1)}, u32[]{:S(2)}, u32[]{:S(2)}) collective-permute-start(bf16[1,512,128]{2,1,0:T(8,128)(2,1)} %get-tuple-element.79), channel_id=1, source_target_pairs={{0,2},{1,3},{2,4},{3,5},{4,6},{5,7},{8,10},{9,11},{10,12},{11,13},... | collective-permute-start | bytes 393224 | tf_op jit(solution)/shard_map/ppermute | solution.py:401
  425.7 7.5 %collective-permute-start.18 = (bf16[1,512,128]{2,1,0:T(8,128)(2,1)}, bf16[1,512,128]{2,1,0:T(8,128)(2,1)}, u32[]{:S(2)}, u32[]{:S(2)}) collective-permute-start(bf16[1,512,128]{2,1,0:T(8,128)(2,1)} %get-tuple-element.80), channel_id=1, source_target_pairs={{2,0},{3,1},{4,2},{5,3},{6,4},{7,5},{10,8},{11,9},{12,10},{13,11},... | collective-permute-start | bytes 393224 | tf_op jit(solution)/shard_map/ppermute | solution.py:401
  439.0 6.1 %collective-permute-start.26 = (bf16[1,128,512]{2,1,0:T(8,128)(2,1)}, bf16[1,128,512]{2,1,0:T(8,128)(2,1)}, u32[]{:S(2)}, u32[]{:S(2)}) collective-permute-start(bf16[1,128,512]{2,1,0:T(8,128)(2,1)} %get-tuple-element.93), channel_id=1, source_target_pairs={{0,8},{8,16},{16,24},{1,9},{9,17},{17,25},{2,10},{10,18},{18,26},{... | collective-permute-start | bytes 393224 | tf_op jit(solution)/shard_map/ppermute | solution.py:394
  442.9 6.6 %collective-permute-start.27 = (bf16[1,128,512]{2,1,0:T(8,128)(2,1)}, bf16[1,128,512]{2,1,0:T(8,128)(2,1)}, u32[]{:S(2)}, u32[]{:S(2)}) collective-permute-start(bf16[1,128,512]{2,1,0:T(8,128)(2,1)} %get-tuple-element.94), channel_id=1, source_target_pairs={{8,0},{16,8},{24,16},{9,1},{17,9},{25,17},{10,2},{18,10},{26,18},{... | collective-permute-start | bytes 393224 | tf_op jit(solution)/shard_map/ppermute | solution.py:394
  453.0 7.5 %collective-permute-start.28 = (bf16[1,512,128]{2,1,0:T(8,128)(2,1)}, bf16[1,512,128]{2,1,0:T(8,128)(2,1)}, u32[]{:S(2)}, u32[]{:S(2)}) collective-permute-start(bf16[1,512,128]{2,1,0:T(8,128)(2,1)} %get-tuple-element.96), channel_id=1, source_target_pairs={{0,2},{1,3},{2,4},{3,5},{4,6},{5,7},{8,10},{9,11},{10,12},{11,13},... | collective-permute-start | bytes 393224 | tf_op jit(solution)/shard_map/ppermute | solution.py:401
  458.0 6.0 %collective-permute-start.29 = (bf16[1,512,128]{2,1,0:T(8,128)(2,1)}, bf16[1,512,128]{2,1,0:T(8,128)(2,1)}, u32[]{:S(2)}, u32[]{:S(2)}) collective-permute-start(bf16[1,512,128]{2,1,0:T(8,128)(2,1)} %get-tuple-element.97), channel_id=1, source_target_pairs={{2,0},{3,1},{4,2},{5,3},{6,4},{7,5},{10,8},{11,9},{12,10},{13,11},... | collective-permute-start | bytes 393224 | tf_op jit(solution)/shard_map/ppermute | solution.py:401
  459.2 12.5 %collective-permute-start.30 = (bf16[1,512,256]{2,1,0:T(8,128)(2,1)}, bf16[1,512,256]{2,1,0:T(8,128)(2,1)}, u32[]{:S(2)}, u32[]{:S(2)}) collective-permute-start(bf16[1,512,256]{2,1,0:T(8,128)(2,1)} %get-tuple-element.99), channel_id=1, source_target_pairs={{0,1},{1,0},{2,3},{3,2},{4,5},{5,4},{6,7},{7,6},{8,9},{9,8},{10,11... | collective-permute-start | bytes 786440 | tf_op jit(solution)/shard_map/ppermute | solution.py:406
  467.5 7.2 %collective-permute-start.31 = (bf16[1,512,256]{2,1,0:T(8,128)(2,1)}, bf16[1,512,256]{2,1,0:T(8,128)(2,1)}, u32[]{:S(2)}, u32[]{:S(2)}) collective-permute-start(bf16[1,512,256]{2,1,0:T(8,128)(2,1)} %get-tuple-element.100), channel_id=1, source_target_pairs={{0,1},{1,0},{2,3},{3,2},{4,5},{5,4},{6,7},{7,6},{8,9},{9,8},{10,11... | collective-permute-start | bytes 786440 | tf_op jit(solution)/shard_map/ppermute | solution.py:406
Sparse Core Ops, SparseCore 0:
  18.7 146.3 reduce-scatter.5
  167.4 77.6 reduce-scatter.9
  247.5 83.2 reduce-scatter.7
  332.9 49.5 reduce-scatter.11
  384.8 51.5 reduce-scatter.13

commit v4 on v3

--- a/solution.py
+++ b/solution.py
@@ -49,16 +49,21 @@
             specs.append(pl.BlockSpec((1, count, rows, wide), lambda s, i: (s, 0, i, 0)))
             plan.append([offset + first + j for offset in offsets for j in range(slots)])
 
+    used = [q for slots_of in plan for q in slots_of]
+    perm = jnp.concatenate([perm[q * sub : (q + 1) * sub] for q in used])
+
     def body(part_ref, perm_ref, *refs):
         out_refs = refs[len(after) :]
         for b in range(rows // sub):
             block = part_ref[0, b * sub : (b + 1) * sub, 0].astype(jnp.float32)
             block = block.reshape(span, wide).astype(jnp.bfloat16)
             moved = jnp.dot(perm_ref[...], block, preferred_element_type=jnp.float32)
-            moved = moved.astype(jnp.bfloat16).reshape(planes, sub, wide)
+            moved = moved.astype(jnp.bfloat16).reshape(len(used), sub, wide)
+            at = 0
             for out_ref, slots_of in zip(out_refs, plan):
-                for n, q in enumerate(slots_of):
-                    out_ref[0, n, b * sub : (b + 1) * sub, :] = moved[q]
+                for n in range(len(slots_of)):
+                    out_ref[0, n, b * sub : (b + 1) * sub, :] = moved[at + n]
+                at += len(slots_of)
 
     return pl.pallas_call(
         body,

time: 486 us -> 487 us (level)
  local copies, waits for them, and re-layouts: 15 us -> 23 us
  waiting for transfers between devices: 252 us -> 246 us
    ppermute x4, waiting for transfers between devices: 146 us -> 139 us  [begin(): added[n] = add_parts(own, lax.ppermute(sent, 'ev', other), after)]
    unnamed x8 -> x18, local copies, waits for them, and re-layouts: 2.85 us -> 8.84 us
  transfers between devices with their start and end apart: 37 -> 37, of which waited for: 22 -> 22; matrix products, arithmetic and copies ran while one was open for 5% -> 7% of each run, Pallas kernels for 21% -> 21%
where the time goes in v4:
time: 487 us; the launch traced here: 485 us
  waiting for transfers between devices  246 us (51%)
  Pallas kernels  121 us (25%)
  starting transfers between devices  69.3 us (14%)
  local copies, waits for them, and re-layouts  23 us (5%)
  between operations  13.4 us (3%)
  other arithmetic  12.9 us (3%)
    ppermute x4, waiting for transfers between devices, begin(): added[n] = add_parts(own, lax.ppermute(sent, 'ev', other), after)  139 us
    ppermute x10, waiting for transfers between devices, cross_x(): ends[n] = (lax.ppermute(high, 'ev', z_up), lax.ppermute(low, 'ev', z_down))  51.2 us
    pallas_call x3, Pallas kernels, split_planes(): pl.pallas_call(body, grid=(shards, slab_x // rows), in_specs=[pl.BlockSpe...  33.5 us
    ppermute x10, starting transfers between devices, cross_x(): ends[n] = (lax.ppermute(high, 'ev', z_up), lax.ppermute(low, 'ev', z_down))  25.5 us
    pallas_call x4, Pallas kernels, add_parts(): pl.pallas_call(body, grid=(shards, slots), in_specs=[spec, spec] + [pl.Bl...  24.4 us
    ppermute x5, starting transfers between devices, divide(): lax.ppermute(bottom, 'gx', x_up)  22 us
    pallas_call x5, Pallas kernels, smooth_x(): pl.pallas_call(body, grid=(slots,), in_specs=[full, edge, edge, pl.BlockS...  21.8 us
    pallas_call x5, Pallas kernels, smooth_y(): pl.pallas_call(body, grid_spec=pltpu.PrefetchScalarGridSpec(num_scalar_pr...  21 us
  transfers between devices with their start and end apart: 37, of which 22 were waited for; matrix products, arithmetic and copies ran while one was open for 7% of the time, Pallas kernels for 21%

profile of v4, /device:TPU:1, one launch (start us, length us, event | category | flops | bytes accessed | tf_op | source)
XLA Modules:
  0.0 485.2 jit_solution(7212039419376143478)
XLA Ops:
  9.3 9.9 %split_planes.3.refs_0_ = bf16[4,4,512,512]{3,2,1,0:T(8,128)(2,1)} custom-call(bf16[1,512,2,8,2048]{4,3,2,1,0:T(8,128)(2,1)} %part_ref.5, bf16[128,256]{1,0:T(8,128)(2,1)} %pad_maximum_fusion.1.perm_ref), custom_call_target="tpu_custom_call" | custom-call | tf_op jit(solution)/shard_map/split_planes/pallas_call | solution.py:68
  26.4 10.5 %split_planes.4 = (bf16[4,2,512,512]{3,2,1,0:T(8,128)(2,1)}, bf16[4,2,512,512]{3,2,1,0:T(8,128)(2,1)}) custom-call(bf16[1,512,2,8,2048]{4,3,2,1,0:T(8,128)(2,1)} %part_ref.5, bf16[128,256]{1,0:T(8,128)(2,1)} %pad_maximum_fusion.perm_ref, bf16[4,4,512,512]{3,2,1,0:T(8,128)(2,1)} %split_planes.3.refs_0_), custom_call_target="tpu_custom_call" | custom-call | tf_op jit(solution)/shard_map/split_planes/pallas_call | solution.py:68
  36.9 11.6 %collective-permute-done.4.refs_2_ = s32[4,256]{1,0:T(4,128)} collective-permute-done((s32[4,256]{1,0:T(4,128)}, s32[4,256]{1,0:T(4,128)}, u32[]{:S(2)}, u32[]{:S(2)}) %collective-permute-start.4) | collective-permute-done | bytes 4128 | tf_op jit(solution)/shard_map/ppermute | solution.py:365
  56.2 13.1 %split_planes.5 = (bf16[4,2,512,512]{3,2,1,0:T(8,128)(2,1)}, bf16[4,2,512,512]{3,2,1,0:T(8,128)(2,1)}, bf16[4,1,512,512]{3,2,1,0:T(8,128)(2,1)}, bf16[4,1,512,51...) custom-call(bf16[1,512,2,8,2048]{4,3,2,1,0:T(8,128)(2,1)} %part_ref.5, ...), custom_call_target="tpu_custom_call" | custom-call | tf_op jit(solution)/shard_map/split_planes/pallas_call | solution.py:68
  69.3 70.2 %collective-permute-done.6.b_ref = bf16[4,2,512,512]{3,2,1,0:T(8,128)(2,1)} collective-permute-done((bf16[4,2,512,512]{3,2,1,0:T(8,128)(2,1)}, bf16[4,2,512,512]{3,2,1,0:T(8,128)(2,1)}, u32[]{:S(2)}, u32[]{:S(2)}) %collective-permute-start.6) | collective-permute-done | bytes 4194336 | tf_op jit(solution)/shard_map/ppermute | solution.py:388
  139.6 7.9 %add_parts.5 = bf16[4,2,512,512]{3,2,1,0:T(8,128)(2,1)} custom-call(bf16[4,2,512,512]{3,2,1,0:T(8,128)(2,1)} %get-tuple-element.53.refs_0_.a_ref, bf16[4,2,512,512]{3,2,1,0:T(8,128)(2,1)} %collective-permute-done.6.b_ref, bf16[4,2,512,512]{3,2,1,0:T(8,128)(2,1)} %get-tuple-element.54.a_ref.refs_0_, bf16[4,1,512,512]{3,2,1,0:T(8,128)(2,1)} %get-tuple-element.59.refs_1_.a_ref, ...), custom_call_target="tpu_custom_call" | custom-call | flops 2097152 | bytes 12582912 | tf_op jit(solution)/shard_map/add_parts/pallas_call | solution.py:109
  148.4 17.4 %reduce-scatter.6.cloned.1.call-done = bf16[1,4,512,512]{3,2,1,0:T(8,128)(2,1)} async-done(((bf16[4,4,512,512]{3,2,1,0:T(8,128)(2,1)}), bf16[1,4,512,512]{3,2,1,0:T(8,128)(2,1)}) %reduce-scatter.6.cloned.1.call-update) | async-done | bytes 2097168 | tf_op jit(solution)/shard_map/reduce_scatter | solution.py:336
  165.8 3.0 slice_bitcast_fusion
  168.8 69.0 %collective-permute-done.b_ref = bf16[4,2,512,512]{3,2,1,0:T(8,128)(2,1)} collective-permute-done((bf16[4,2,512,512]{3,2,1,0:T(8,128)(2,1)}, bf16[4,2,512,512]{3,2,1,0:T(8,128)(2,1)}, u32[]{:S(2)}, u32[]{:S(2)}) %collective-permute-start) | collective-permute-done | bytes 4194336 | tf_op jit(solution)/shard_map/ppermute | solution.py:388
  237.8 7.9 %add_parts.4 = bf16[4,2,512,512]{3,2,1,0:T(8,128)(2,1)} custom-call(bf16[4,2,512,512]{3,2,1,0:T(8,128)(2,1)} %get-tuple-element.54.a_ref.refs_0_, bf16[4,2,512,512]{3,2,1,0:T(8,128)(2,1)} %collective-permute-done.b_ref, bf16[2,512,512]{2,1,0:T(8,128)(2,1)} %get-tuple-element.102.refs_0_), custom_call_target="tpu_custom_call" | custom-call | flops 2097152 | bytes 12582912 | tf_op jit(solution)/shard_map/add_parts/pallas_call | solution.py:109
  251.5 3.2 add_convert_fusion.tiles_ref
  254.7 3.4 scale.6
  258.1 6.1 %collective-permute-start.7 = (bf16[2,128,512]{2,1,0:T(8,128)(2,1)}, bf16[2,128,512]{2,1,0:T(8,128)(2,1)}, u32[]{:S(2)}, u32[]{:S(2)}) collective-permute-start(bf16[2,128,512]{2,1,0:T(8,128)(2,1)} %get-tuple-element.64), channel_id=1, source_target_pairs={{0,8},{8,16},{16,24},{1,9},{9,17},{17,25},{2,10},{10,18},{18,26},{... | collective-permute-start | bytes 786440 | tf_op jit(solution)/shard_map/ppermute | solution.py:399
  266.2 2.9 fusion.9
  272.6 5.0 %smooth_x.5 = (bf16[2,512,512]{2,1,0:T(8,128)(2,1)}, bf16[2,512,128]{2,1,0:T(8,128)(2,1)}, bf16[2,512,128]{2,1,0:T(8,128)(2,1)}) custom-call(bf16[2,512,512]{2,1,0:T(8,128)(2,1)} %get-tuple-element.63.mid_ref, bf16[2,128,512]{2,1,0:T(8,128)(2,1)} %collective-permute-done.7.before_ref, bf16[2,128,512]{2,1,0:T(8,128)(2,1)} %collective-permute-done.8.after_ref, ...), custom_call_target="tpu_custom_call" | custom-call | flops 1610612736 | bytes 3145728 | tf_op jit(solution)/shard_map/smooth_x/pallas_call | solution.py:202
  277.6 3.9 collective-permute-start.9
  283.3 3.2 fusion.16.tiles_ref
  288.5 3.6 collective-permute-done.9.before_ref
  292.1 10.8 %collective-permute-done.10.after_ref = bf16[2,512,128]{2,1,0:T(8,128)(2,1)} collective-permute-done((bf16[2,512,128]{2,1,0:T(8,128)(2,1)}, bf16[2,512,128]{2,1,0:T(8,128)(2,1)}, u32[]{:S(2)}, u32[]{:S(2)}) %collective-permute-start.10) | collective-permute-done | bytes 262176 | tf_op jit(solution)/shard_map/ppermute | solution.py:406
  302.9 4.7 smooth_y.5
  307.6 5.1 %collective-permute-done.11.refs_1_ = bf16[2,512,512]{2,1,0:T(8,128)(2,1)} collective-permute-done((bf16[2,512,512]{2,1,0:T(8,128)(2,1)}, bf16[2,512,512]{2,1,0:T(8,128)(2,1)}, u32[]{:S(2)}, u32[]{:S(2)}) %collective-permute-start.11) | collective-permute-done | bytes 1048608 | tf_op jit(solution)/shard_map/ppermute | solution.py:392
  312.7 4.3 add_parts.6
  317.2 3.2 scale.8
  320.4 7.5 %collective-permute-start.20 = (bf16[2,128,512]{2,1,0:T(8,128)(2,1)}, bf16[2,128,512]{2,1,0:T(8,128)(2,1)}, u32[]{:S(2)}, u32[]{:S(2)}) collective-permute-start(bf16[2,128,512]{2,1,0:T(8,128)(2,1)} %get-tuple-element.84), channel_id=1, source_target_pairs={{0,8},{8,16},{16,24},{1,9},{9,17},{17,25},{2,10},{10,18},{18,26},{... | collective-permute-start | bytes 786440 | tf_op jit(solution)/shard_map/ppermute | solution.py:399
  331.5 4.7 collective-permute-done.21.after_ref
  336.2 4.8 smooth_x.8
  341.0 3.9 collective-permute-start.22
  346.2 8.6 %collective-permute-done.22.before_ref = bf16[2,512,128]{2,1,0:T(8,128)(2,1)} collective-permute-done((bf16[2,512,128]{2,1,0:T(8,128)(2,1)}, bf16[2,512,128]{2,1,0:T(8,128)(2,1)}, u32[]{:S(2)}, u32[]{:S(2)}) %collective-permute-start.22) | collective-permute-done | bytes 262176 | tf_op jit(solution)/shard_map/ppermute | solution.py:406
  354.8 11.1 %collective-permute-done.23.after_ref = bf16[2,512,128]{2,1,0:T(8,128)(2,1)} collective-permute-done((bf16[2,512,128]{2,1,0:T(8,128)(2,1)}, bf16[2,512,128]{2,1,0:T(8,128)(2,1)}, u32[]{:S(2)}, u32[]{:S(2)}) %collective-permute-start.23) | collective-permute-done | bytes 262176 | tf_op jit(solution)/shard_map/ppermute | solution.py:406
  365.9 4.7 smooth_y.8
  370.5 4.3 add_parts.7
  388.3 4.8 smooth_x.6
  393.1 3.7 collective-permute-start.13
  400.1 2.9 collective-permute-start.16
  407.0 3.5 smooth_x.7
  410.5 7.3 %collective-permute-done.14.after_ref = bf16[2,512,128]{2,1,0:T(8,128)(2,1)} collective-permute-done((bf16[2,512,128]{2,1,0:T(8,128)(2,1)}, bf16[2,512,128]{2,1,0:T(8,128)(2,1)}, u32[]{:S(2)}, u32[]{:S(2)}) %collective-permute-start.14) | collective-permute-done | bytes 262176 | tf_op jit(solution)/shard_map/ppermute | solution.py:406
  417.8 4.7 smooth_y.6
  427.7 4.5 collective-permute-done.17.before_ref
  434.0 3.5 smooth_y.7
  439.8 3.8 collective-permute-start.26
  445.9 4.4 collective-permute-done.27.after_ref
  450.3 3.5 smooth_x.9
  453.8 4.9 %collective-permute-start.28 = (bf16[1,512,128]{2,1,0:T(8,128)(2,1)}, bf16[1,512,128]{2,1,0:T(8,128)(2,1)}, u32[]{:S(2)}, u32[]{:S(2)}) collective-permute-start(bf16[1,512,128]{2,1,0:T(8,128)(2,1)} %get-tuple-element.96), channel_id=1, source_target_pairs={{0,2},{1,3},{2,4},{3,5},{4,6},{5,7},{8,10},{9,11},{10,12},{11,13},... | collective-permute-start | bytes 393224 | tf_op jit(solution)/shard_map/ppermute | solution.py:406
  461.3 3.5 collective-permute-done.29.after_ref
  464.8 3.5 smooth_y.9
  469.4 3.1 join_planes.2.refs_7_
  472.5 2.9 collective-permute-done.31.refs_5_
  475.5 3.2 join_planes.3
  (98 shorter events, 74.5 us)
Async XLA Ops:
  6.5 159.3 %reduce-scatter.6.cloned.1.call-start = ((), (), s32[]{:S(2)}) async-start(), calls=%async_computation.5 | async-start | bytes 10485760 | tf_op jit(solution)/shard_map/reduce_scatter | solution.py:336
  7.4 0.7 copy-start
  19.3 5.9 %copy-start.3 = (s32[8,256]{1,0:T(8,128)S(1)}, s32[8,256]{1,0:T(8,128)}, u32[]{:S(2)}) copy-start(s32[8,256]{1,0:T(8,128)} %param.8) | copy-start | bytes 24580
  19.3 6.5 %copy-start.1 = (bf16[64,256]{1,0:T(8,128)(2,1)S(1)}, bf16[64,256]{1,0:T(8,128)(2,1)}, u32[]{:S(2)}) copy-start(bf16[64,256]{1,0:T(8,128)(2,1)} %get-tuple-element.105) | copy-start | bytes 98308
  19.3 6.4 %copy-start.2 = (bf16[64,256]{1,0:T(8,128)(2,1)S(1)}, bf16[64,256]{1,0:T(8,128)(2,1)}, u32[]{:S(2)}) copy-start(bf16[64,256]{1,0:T(8,128)(2,1)} %get-tuple-element.106) | copy-start | bytes 98308
  19.3 235.4 %reduce-scatter.10.cloned.1.call-start = ((), (), s32[]{:S(2)}) async-start(), calls=%async_computation.7 | async-start | bytes 5242880 | tf_op jit(solution)/shard_map/reduce_scatter | solution.py:336
  23.1 25.4 %collective-permute-start.1 = (bf16[4,512,256]{2,1,0:T(8,128)(2,1)}, bf16[4,512,256]{2,1,0:T(8,128)(2,1)}, u32[]{:S(2)}, u32[]{:S(2)}) collective-permute-start(bf16[4,512,256]{2,1,0:T(8,128)(2,1)} %bitcast.18), channel_id=1, source_target_pairs={{0,1},{1,0},{2,3},{3,2},{4,5},{5,4},{6,7},{7,6},{8,9},{9,8},{10,11... | collective-permute-start | bytes 3145736 | tf_op jit(solution)/shard_map/ppermute | solution.py:352
  25.7 22.7 %collective-permute-start.4 = (s32[4,256]{1,0:T(4,128)}, s32[4,256]{1,0:T(4,128)}, u32[]{:S(2)}, u32[]{:S(2)}) collective-permute-start(s32[4,256]{1,0:T(4,128)} %get-tuple-element.109), channel_id=1, source_target_pairs={{0,1},{1,0},{2,3},{3,2},{4,5},{5,4},{6,7},{7,6},{8,9},{9,8},{10,11... | collective-permute-start | bytes 12296 | tf_op jit(solution)/shard_map/ppermute | solution.py:365
  48.4 91.2 %collective-permute-start.6 = (bf16[4,2,512,512]{3,2,1,0:T(8,128)(2,1)}, bf16[4,2,512,512]{3,2,1,0:T(8,128)(2,1)}, u32[]{:S(2)}, u32[]{:S(2)}) collective-permute-start(bf16[4,2,512,512]{3,2,1,0:T(8,128)(2,1)} %hold.1), channel_id=1, source_target_pairs={{0,1},{1,0},{2,3},{3,2},{4,5},{5,4},{6,7},{7,6},{8,9},{9,8},{10,11... | collective-permute-start | bytes 12582920 | tf_op jit(solution)/shard_map/ppermute | solution.py:388
  147.5 227.5 %reduce-scatter.8.cloned.1.call-start = ((), (), s32[]{:S(2)}) async-start(), calls=%async_computation.6 | async-start | bytes 5242880 | tf_op jit(solution)/shard_map/reduce_scatter | solution.py:336
  147.6 90.3 %collective-permute-start = (bf16[4,2,512,512]{3,2,1,0:T(8,128)(2,1)}, bf16[4,2,512,512]{3,2,1,0:T(8,128)(2,1)}, u32[]{:S(2)}, u32[]{:S(2)}) collective-permute-start(bf16[4,2,512,512]{3,2,1,0:T(8,128)(2,1)} %get-tuple-element.55), channel_id=1, source_target_pairs={{0,1},{1,0},{2,3},{3,2},{4,5},{5,4},{6,7},{7,6},{8,9},{9,8},{10,11... | collective-permute-start | bytes 12582920 | tf_op jit(solution)/shard_map/ppermute | solution.py:388
  245.7 138.9 %reduce-scatter.12.cloned.1.call-start = ((), (), s32[]{:S(2)}) async-start(), calls=%async_computation.8 | async-start | bytes 2621440 | tf_op jit(solution)/shard_map/reduce_scatter | solution.py:336
  245.8 61.8 %collective-permute-start.5 = (bf16[4,1,512,512]{3,2,1,0:T(8,128)(2,1)}, bf16[4,1,512,512]{3,2,1,0:T(8,128)(2,1)}, u32[]{:S(2)}, u32[]{:S(2)}) collective-permute-start(bf16[4,1,512,512]{3,2,1,0:T(8,128)(2,1)} %get-tuple-element.60), channel_id=1, source_target_pairs={{0,1},{1,0},{2,3},{3,2},{4,5},{5,4},{6,7},{7,6},{8,9},{9,8},{10,11... | collective-permute-start | bytes 6291464 | tf_op jit(solution)/shard_map/ppermute | solution.py:388
  248.7 2.3 copy-start.4
  248.7 2.3 copy-start.5
  258.1 12.9 %collective-permute-start.7 = (bf16[2,128,512]{2,1,0:T(8,128)(2,1)}, bf16[2,128,512]{2,1,0:T(8,128)(2,1)}, u32[]{:S(2)}, u32[]{:S(2)}) collective-permute-start(bf16[2,128,512]{2,1,0:T(8,128)(2,1)} %get-tuple-element.64), channel_id=1, source_target_pairs={{0,8},{8,16},{16,24},{1,9},{9,17},{17,25},{2,10},{10,18},{18,26},{... | collective-permute-start | bytes 786440 | tf_op jit(solution)/shard_map/ppermute | solution.py:399
  264.3 8.3 %collective-permute-start.8 = (bf16[2,128,512]{2,1,0:T(8,128)(2,1)}, bf16[2,128,512]{2,1,0:T(8,128)(2,1)}, u32[]{:S(2)}, u32[]{:S(2)}) collective-permute-start(bf16[2,128,512]{2,1,0:T(8,128)(2,1)} %get-tuple-element.65), channel_id=1, source_target_pairs={{8,0},{16,8},{24,16},{9,1},{17,9},{25,17},{10,2},{18,10},{26,18},{... | collective-permute-start | bytes 786440 | tf_op jit(solution)/shard_map/ppermute | solution.py:399
  277.6 14.5 %collective-permute-start.9 = (bf16[2,512,128]{2,1,0:T(8,128)(2,1)}, bf16[2,512,128]{2,1,0:T(8,128)(2,1)}, u32[]{:S(2)}, u32[]{:S(2)}) collective-permute-start(bf16[2,512,128]{2,1,0:T(8,128)(2,1)} %get-tuple-element.67), channel_id=1, source_target_pairs={{0,2},{1,3},{2,4},{3,5},{4,6},{5,7},{8,10},{9,11},{10,12},{11,13},... | collective-permute-start | bytes 786440 | tf_op jit(solution)/shard_map/ppermute | solution.py:406
  281.5 21.4 %collective-permute-start.10 = (bf16[2,512,128]{2,1,0:T(8,128)(2,1)}, bf16[2,512,128]{2,1,0:T(8,128)(2,1)}, u32[]{:S(2)}, u32[]{:S(2)}) collective-permute-start(bf16[2,512,128]{2,1,0:T(8,128)(2,1)} %get-tuple-element.68), channel_id=1, source_target_pairs={{2,0},{3,1},{4,2},{5,3},{6,4},{7,5},{10,8},{11,9},{12,10},{13,11},... | collective-permute-start | bytes 786440 | tf_op jit(solution)/shard_map/ppermute | solution.py:406
  283.0 29.8 %collective-permute-start.11 = (bf16[2,512,512]{2,1,0:T(8,128)(2,1)}, bf16[2,512,512]{2,1,0:T(8,128)(2,1)}, u32[]{:S(2)}, u32[]{:S(2)}) collective-permute-start(bf16[2,512,512]{2,1,0:T(8,128)(2,1)} %get-tuple-element.101), channel_id=1, source_target_pairs={{0,1},{1,0},{2,3},{3,2},{4,5},{5,4},{6,7},{7,6},{8,9},{9,8},{10,11... | collective-permute-start | bytes 3145736 | tf_op jit(solution)/shard_map/ppermute | solution.py:392
  317.1 120.4 %reduce-scatter.14.cloned.1.call-start = ((), (), s32[]{:S(2)}) async-start(), calls=%async_computation.9 | async-start | bytes 2621440 | tf_op jit(solution)/shard_map/reduce_scatter | solution.py:336
  317.1 53.4 %collective-permute-start.19 = (bf16[4,1,512,512]{3,2,1,0:T(8,128)(2,1)}, bf16[4,1,512,512]{3,2,1,0:T(8,128)(2,1)}, u32[]{:S(2)}, u32[]{:S(2)}) collective-permute-start(bf16[4,1,512,512]{3,2,1,0:T(8,128)(2,1)} %get-tuple-element.82), channel_id=1, source_target_pairs={{0,1},{1,0},{2,3},{3,2},{4,5},{5,4},{6,7},{7,6},{8,9},{9,8},{10,11... | collective-permute-start | bytes 6291464 | tf_op jit(solution)/shard_map/ppermute | solution.py:388
  320.4 11.1 %collective-permute-start.20 = (bf16[2,128,512]{2,1,0:T(8,128)(2,1)}, bf16[2,128,512]{2,1,0:T(8,128)(2,1)}, u32[]{:S(2)}, u32[]{:S(2)}) collective-permute-start(bf16[2,128,512]{2,1,0:T(8,128)(2,1)} %get-tuple-element.84), channel_id=1, source_target_pairs={{0,8},{8,16},{16,24},{1,9},{9,17},{17,25},{2,10},{10,18},{18,26},{... | collective-permute-start | bytes 786440 | tf_op jit(solution)/shard_map/ppermute | solution.py:399
  327.9 8.3 %collective-permute-start.21 = (bf16[2,128,512]{2,1,0:T(8,128)(2,1)}, bf16[2,128,512]{2,1,0:T(8,128)(2,1)}, u32[]{:S(2)}, u32[]{:S(2)}) collective-permute-start(bf16[2,128,512]{2,1,0:T(8,128)(2,1)} %get-tuple-element.85), channel_id=1, source_target_pairs={{8,0},{16,8},{24,16},{9,1},{17,9},{25,17},{10,2},{18,10},{26,18},{... | collective-permute-start | bytes 786440 | tf_op jit(solution)/shard_map/ppermute | solution.py:399
  341.0 13.8 %collective-permute-start.22 = (bf16[2,512,128]{2,1,0:T(8,128)(2,1)}, bf16[2,512,128]{2,1,0:T(8,128)(2,1)}, u32[]{:S(2)}, u32[]{:S(2)}) collective-permute-start(bf16[2,512,128]{2,1,0:T(8,128)(2,1)} %get-tuple-element.87), channel_id=1, source_target_pairs={{0,2},{1,3},{2,4},{3,5},{4,6},{5,7},{8,10},{9,11},{10,12},{11,13},... | collective-permute-start | bytes 786440 | tf_op jit(solution)/shard_map/ppermute | solution.py:406
  344.9 20.9 %collective-permute-start.23 = (bf16[2,512,128]{2,1,0:T(8,128)(2,1)}, bf16[2,512,128]{2,1,0:T(8,128)(2,1)}, u32[]{:S(2)}, u32[]{:S(2)}) collective-permute-start(bf16[2,512,128]{2,1,0:T(8,128)(2,1)} %get-tuple-element.88), channel_id=1, source_target_pairs={{2,0},{3,1},{4,2},{5,3},{6,4},{7,5},{10,8},{11,9},{12,10},{13,11},... | collective-permute-start | bytes 786440 | tf_op jit(solution)/shard_map/ppermute | solution.py:406
  374.9 9.7 %collective-permute-start.12 = (bf16[2,512,256]{2,1,0:T(8,128)(2,1)}, bf16[2,512,256]{2,1,0:T(8,128)(2,1)}, u32[]{:S(2)}, u32[]{:S(2)}) collective-permute-start(bf16[2,512,256]{2,1,0:T(8,128)(2,1)} %get-tuple-element.70), channel_id=1, source_target_pairs={{0,1},{1,0},{2,3},{3,2},{4,5},{5,4},{6,7},{7,6},{8,9},{9,8},{10,11... | collective-permute-start | bytes 1572872 | tf_op jit(solution)/shard_map/ppermute | solution.py:411
  377.7 9.2 %collective-permute-start.2 = (bf16[2,128,512]{2,1,0:T(8,128)(2,1)}, bf16[2,128,512]{2,1,0:T(8,128)(2,1)}, u32[]{:S(2)}, u32[]{:S(2)}) collective-permute-start(bf16[2,128,512]{2,1,0:T(8,128)(2,1)} %get-tuple-element.57), channel_id=1, source_target_pairs={{0,8},{8,16},{16,24},{1,9},{9,17},{17,25},{2,10},{10,18},{18,26},{... | collective-permute-start | bytes 786440 | tf_op jit(solution)/shard_map/ppermute | solution.py:399
  380.3 8.0 %collective-permute-start.3 = (bf16[2,128,512]{2,1,0:T(8,128)(2,1)}, bf16[2,128,512]{2,1,0:T(8,128)(2,1)}, u32[]{:S(2)}, u32[]{:S(2)}) collective-permute-start(bf16[2,128,512]{2,1,0:T(8,128)(2,1)} %get-tuple-element.58), channel_id=1, source_target_pairs={{8,0},{16,8},{24,16},{9,1},{17,9},{25,17},{10,2},{18,10},{26,18},{... | collective-permute-start | bytes 786440 | tf_op jit(solution)/shard_map/ppermute | solution.py:399
  393.1 17.4 %collective-permute-start.13 = (bf16[2,512,128]{2,1,0:T(8,128)(2,1)}, bf16[2,512,128]{2,1,0:T(8,128)(2,1)}, u32[]{:S(2)}, u32[]{:S(2)}) collective-permute-start(bf16[2,512,128]{2,1,0:T(8,128)(2,1)} %get-tuple-element.73), channel_id=1, source_target_pairs={{0,2},{1,3},{2,4},{3,5},{4,6},{5,7},{8,10},{9,11},{10,12},{11,13},... | collective-permute-start | bytes 786440 | tf_op jit(solution)/shard_map/ppermute | solution.py:406
  396.8 21.1 %collective-permute-start.14 = (bf16[2,512,128]{2,1,0:T(8,128)(2,1)}, bf16[2,512,128]{2,1,0:T(8,128)(2,1)}, u32[]{:S(2)}, u32[]{:S(2)}) collective-permute-start(bf16[2,512,128]{2,1,0:T(8,128)(2,1)} %get-tuple-element.74), channel_id=1, source_target_pairs={{2,0},{3,1},{4,2},{5,3},{6,4},{7,5},{10,8},{11,9},{12,10},{13,11},... | collective-permute-start | bytes 786440 | tf_op jit(solution)/shard_map/ppermute | solution.py:406
  398.0 6.7 %collective-permute-start.15 = (bf16[1,128,512]{2,1,0:T(8,128)(2,1)}, bf16[1,128,512]{2,1,0:T(8,128)(2,1)}, u32[]{:S(2)}, u32[]{:S(2)}) collective-permute-start(bf16[1,128,512]{2,1,0:T(8,128)(2,1)} %get-tuple-element.75), channel_id=1, source_target_pairs={{0,8},{8,16},{16,24},{1,9},{9,17},{17,25},{2,10},{10,18},{18,26},{... | collective-permute-start | bytes 393224 | tf_op jit(solution)/shard_map/ppermute | solution.py:399
  400.1 6.9 %collective-permute-start.16 = (bf16[1,128,512]{2,1,0:T(8,128)(2,1)}, bf16[1,128,512]{2,1,0:T(8,128)(2,1)}, u32[]{:S(2)}, u32[]{:S(2)}) collective-permute-start(bf16[1,128,512]{2,1,0:T(8,128)(2,1)} %get-tuple-element.76), channel_id=1, source_target_pairs={{8,0},{16,8},{24,16},{9,1},{17,9},{25,17},{10,2},{18,10},{26,18},{... | collective-permute-start | bytes 393224 | tf_op jit(solution)/shard_map/ppermute | solution.py:399
  403.0 34.5 %collective-permute-start.24 = (bf16[2,512,256]{2,1,0:T(8,128)(2,1)}, bf16[2,512,256]{2,1,0:T(8,128)(2,1)}, u32[]{:S(2)}, u32[]{:S(2)}) collective-permute-start(bf16[2,512,256]{2,1,0:T(8,128)(2,1)} %get-tuple-element.90), channel_id=1, source_target_pairs={{0,1},{1,0},{2,3},{3,2},{4,5},{5,4},{6,7},{7,6},{8,9},{9,8},{10,11... | collective-permute-start | bytes 1572872 | tf_op jit(solution)/shard_map/ppermute | solution.py:411
  422.5 15.0 %collective-permute-start.25 = (bf16[2,512,256]{2,1,0:T(8,128)(2,1)}, bf16[2,512,256]{2,1,0:T(8,128)(2,1)}, u32[]{:S(2)}, u32[]{:S(2)}) collective-permute-start(bf16[2,512,256]{2,1,0:T(8,128)(2,1)} %get-tuple-element.91), channel_id=1, source_target_pairs={{0,1},{1,0},{2,3},{3,2},{4,5},{5,4},{6,7},{7,6},{8,9},{9,8},{10,11... | collective-permute-start | bytes 1572872 | tf_op jit(solution)/shard_map/ppermute | solution.py:411
  423.8 8.4 %collective-permute-start.17 = (bf16[1,512,128]{2,1,0:T(8,128)(2,1)}, bf16[1,512,128]{2,1,0:T(8,128)(2,1)}, u32[]{:S(2)}, u32[]{:S(2)}) collective-permute-start(bf16[1,512,128]{2,1,0:T(8,128)(2,1)} %get-tuple-element.79), channel_id=1, source_target_pairs={{0,2},{1,3},{2,4},{3,5},{4,6},{5,7},{8,10},{9,11},{10,12},{11,13},... | collective-permute-start | bytes 393224 | tf_op jit(solution)/shard_map/ppermute | solution.py:406
  426.4 7.6 %collective-permute-start.18 = (bf16[1,512,128]{2,1,0:T(8,128)(2,1)}, bf16[1,512,128]{2,1,0:T(8,128)(2,1)}, u32[]{:S(2)}, u32[]{:S(2)}) collective-permute-start(bf16[1,512,128]{2,1,0:T(8,128)(2,1)} %get-tuple-element.80), channel_id=1, source_target_pairs={{2,0},{3,1},{4,2},{5,3},{6,4},{7,5},{10,8},{11,9},{12,10},{13,11},... | collective-permute-start | bytes 393224 | tf_op jit(solution)/shard_map/ppermute | solution.py:406
  439.8 6.1 %collective-permute-start.26 = (bf16[1,128,512]{2,1,0:T(8,128)(2,1)}, bf16[1,128,512]{2,1,0:T(8,128)(2,1)}, u32[]{:S(2)}, u32[]{:S(2)}) collective-permute-start(bf16[1,128,512]{2,1,0:T(8,128)(2,1)} %get-tuple-element.93), channel_id=1, source_target_pairs={{0,8},{8,16},{16,24},{1,9},{9,17},{17,25},{2,10},{10,18},{18,26},{... | collective-permute-start | bytes 393224 | tf_op jit(solution)/shard_map/ppermute | solution.py:399
  443.7 6.6 %collective-permute-start.27 = (bf16[1,128,512]{2,1,0:T(8,128)(2,1)}, bf16[1,128,512]{2,1,0:T(8,128)(2,1)}, u32[]{:S(2)}, u32[]{:S(2)}) collective-permute-start(bf16[1,128,512]{2,1,0:T(8,128)(2,1)} %get-tuple-element.94), channel_id=1, source_target_pairs={{8,0},{16,8},{24,16},{9,1},{17,9},{25,17},{10,2},{18,10},{26,18},{... | collective-permute-start | bytes 393224 | tf_op jit(solution)/shard_map/ppermute | solution.py:399
  453.8 7.5 %collective-permute-start.28 = (bf16[1,512,128]{2,1,0:T(8,128)(2,1)}, bf16[1,512,128]{2,1,0:T(8,128)(2,1)}, u32[]{:S(2)}, u32[]{:S(2)}) collective-permute-start(bf16[1,512,128]{2,1,0:T(8,128)(2,1)} %get-tuple-element.96), channel_id=1, source_target_pairs={{0,2},{1,3},{2,4},{3,5},{4,6},{5,7},{8,10},{9,11},{10,12},{11,13},... | collective-permute-start | bytes 393224 | tf_op jit(solution)/shard_map/ppermute | solution.py:406
  458.7 6.0 %collective-permute-start.29 = (bf16[1,512,128]{2,1,0:T(8,128)(2,1)}, bf16[1,512,128]{2,1,0:T(8,128)(2,1)}, u32[]{:S(2)}, u32[]{:S(2)}) collective-permute-start(bf16[1,512,128]{2,1,0:T(8,128)(2,1)} %get-tuple-element.97), channel_id=1, source_target_pairs={{2,0},{3,1},{4,2},{5,3},{6,4},{7,5},{10,8},{11,9},{12,10},{13,11},... | collective-permute-start | bytes 393224 | tf_op jit(solution)/shard_map/ppermute | solution.py:406
  460.0 12.5 %collective-permute-start.30 = (bf16[1,512,256]{2,1,0:T(8,128)(2,1)}, bf16[1,512,256]{2,1,0:T(8,128)(2,1)}, u32[]{:S(2)}, u32[]{:S(2)}) collective-permute-start(bf16[1,512,256]{2,1,0:T(8,128)(2,1)} %get-tuple-element.99), channel_id=1, source_target_pairs={{0,1},{1,0},{2,3},{3,2},{4,5},{5,4},{6,7},{7,6},{8,9},{9,8},{10,11... | collective-permute-start | bytes 786440 | tf_op jit(solution)/shard_map/ppermute | solution.py:411
  468.2 7.2 %collective-permute-start.31 = (bf16[1,512,256]{2,1,0:T(8,128)(2,1)}, bf16[1,512,256]{2,1,0:T(8,128)(2,1)}, u32[]{:S(2)}, u32[]{:S(2)}) collective-permute-start(bf16[1,512,256]{2,1,0:T(8,128)(2,1)} %get-tuple-element.100), channel_id=1, source_target_pairs={{0,1},{1,0},{2,3},{3,2},{4,5},{5,4},{6,7},{7,6},{8,9},{9,8},{10,11... | collective-permute-start | bytes 786440 | tf_op jit(solution)/shard_map/ppermute | solution.py:411
Sparse Core Ops, SparseCore 0:
  19.4 146.3 reduce-scatter.5
  168.1 77.6 reduce-scatter.9
  248.2 83.2 reduce-scatter.7
  333.7 49.5 reduce-scatter.11
  385.6 51.5 reduce-scatter.13
